TPU v7x, 512 devices: a whole 4x8x8 slice. The times are simulated.
512 devices in a mesh: prefix: 32 (over y_lo, z, core), resp: 16 (over x, y_hi).
Axes of the slice: x: 4, y: 8 (y_hi: 4, y_lo: 2; y = y_hi * 2 + y_lo), z: 8, core: 2. Of those that a mesh axis runs over, the one named last changes fastest.
Arguments:
- prefix_q: bfloat16 [4096, 8192], P('prefix', 'resp'), may hold values from -0.1796875 to 0.1796875
- prefix_k: bfloat16 [4096, 8192], P('prefix', 'resp'), may hold values from -0.08984375 to 0.08984375
- prefix_v: bfloat16 [4096, 8192], P('prefix', 'resp'), may hold values from -6 to 6
- prefix_dout: bfloat16 [4096, 8192], P('prefix', 'resp'), may hold values from -3 to 3
- resp_q: bfloat16 [16, 256, 8192], P('resp', None, 'prefix'), may hold values from -0.1796875 to 0.1796875
- resp_k: bfloat16 [16, 256, 8192], P('resp', None, 'prefix'), may hold values from -0.1796875 to 0.1796875
- resp_v: bfloat16 [16, 256, 8192], P('resp', None, 'prefix'), may hold values from -6 to 6
- resp_dout: bfloat16 [16, 256, 8192], P('resp', None, 'prefix'), may hold values from -0.75 to 0.75
- resp_lengths: int32 [16], P('resp'), may hold values from 128 to 256, as said below
- decay_exps: int32 [64], replicated, may hold values from 5120 to 16383
Outputs:
- prefix_dq: bfloat16 [4096, 8192], P('prefix', 'resp')
- prefix_dk: bfloat16 [4096, 8192], P('prefix', 'resp')
- prefix_dv: bfloat16 [4096, 8192], P('prefix', 'resp')
- resp_dq: bfloat16 [16, 256, 8192], P('resp', None, 'prefix')
- resp_dk: bfloat16 [16, 256, 8192], P('resp', None, 'prefix')
- resp_dv: bfloat16 [16, 256, 8192], P('resp', None, 'prefix')
Inputs may be any that keep to these rules, and one draw needn't show every extreme that they name: `resp_lengths`: each length is a multiple of 128; some response has exactly 256 tokens.
All inputs are finite; a program needn't handle non-finite values.
Results may differ from a plain program's by a relative error of at most 0.0057.
Values may be sent and summed in bfloat16 or wider, within the bound.
No kernel may reach another device: no remote copies, remote signals or barrier semaphores. Data moves between devices by JAX's collectives and lax.ppermute only.
A program may use at most 128 MiB of HBM per device.

v0:
```python
import jax
import jax.numpy as jnp
from jax import lax
from jax.sharding import PartitionSpec as P

D = 128
STRETCH = 128


def carried_in(value, axis, join, neutral, backward):
    count, mine = (lax.axis_size(axis), lax.axis_index(axis))
    pieces = jax.tree.map(lambda part: lax.all_gather(part, axis), value)
    if backward:
        pieces = jax.tree.map(lambda part: part[::-1], pieces)
        mine = count - 1 - mine
    total = jax.tree.map(
        lambda part, zero: jnp.full_like(part, 0) + jnp.asarray(zero, part.dtype), value, neutral
    )

    def turn(position, total):
        longer = join(total, jax.tree.map(lambda part: part[position], pieces))
        return jax.tree.map(lambda new, old: jnp.where(position < mine, new, old), longer, total)

    return lax.fori_loop(0, count - 1, turn, total)


def spread(x, axis, root):
    mine = lax.axis_index(axis) == root
    return lax.psum(jnp.where(mine, x, jnp.zeros_like(x)), axis)


def decay_matrix(decay_rates, count):
    places = jnp.arange(count)
    offsets = (places[:, None] - places[None, :]).astype(jnp.float32)
    return jnp.where(
        offsets[None] >= 0.0,
        jnp.exp(-decay_rates[:, None, None] * jnp.maximum(offsets, 0.0)[None]),
        0.0,
    )


def local_grads(queries, keys_in, values, grad_out, decay_rates):
    decay_mask = decay_matrix(decay_rates, queries.shape[0])
    scores = jnp.einsum("thd,shd->hts", queries, keys_in, preferred_element_type=jnp.float32)
    weights = (scores * decay_mask).astype(jnp.bfloat16)
    dscores = (
        jnp.einsum("thd,shd->hts", grad_out, values, preferred_element_type=jnp.float32)
        * decay_mask
    ).astype(jnp.bfloat16)
    grad_q = jnp.einsum("hts,shd->thd", dscores, keys_in, preferred_element_type=jnp.float32)
    grad_k = jnp.einsum("hts,thd->shd", dscores, queries, preferred_element_type=jnp.float32)
    grad_v = jnp.einsum("hts,thd->shd", weights, grad_out, preferred_element_type=jnp.float32)
    return (grad_q, grad_k, grad_v)


def weighted_outer(left, weight, right):
    scaled = (left * weight[..., None]).astype(jnp.bfloat16)
    return jnp.einsum("...thd,...the->...hde", scaled, right, preferred_element_type=jnp.float32)


def chain_combine(former, latter):
    return (former[0] * latter[1][:, None, None] + latter[0], former[1] * latter[1])


def local(
    prefix_q,
    prefix_k,
    prefix_v,
    prefix_dout,
    resp_q,
    resp_k,
    resp_v,
    resp_dout,
    resp_lengths,
    decay_exps,
):
    chain = lax.axis_size("prefix")
    link = lax.axis_index("prefix")
    column = lax.axis_index("resp")
    tract = prefix_q.shape[0]
    group = prefix_q.shape[1] // D
    pair = resp_q.shape[2] // D
    span = resp_q.shape[1]
    all_rates = jnp.exp2(-decay_exps.astype(jnp.float32) / 1024.0)
    pre_rates = lax.dynamic_slice_in_dim(all_rates, column * group, group)
    resp_rates = lax.dynamic_slice_in_dim(all_rates, link * pair, pair)
    pre_shape = (tract, group, D)
    pre_q = prefix_q.reshape(pre_shape)
    pre_k = prefix_k.reshape(pre_shape)
    pre_v = prefix_v.reshape(pre_shape)
    pre_g = prefix_dout.reshape(pre_shape)
    places = jnp.arange(tract).astype(jnp.float32)
    key_weight = jnp.exp(-pre_rates[None, :] * (tract - 1.0 - places)[:, None])
    query_weight = jnp.exp(-pre_rates[None, :] * places[:, None])
    tract_kv = weighted_outer(pre_k, key_weight, pre_v)
    tract_qd = weighted_outer(pre_q, query_weight, pre_g)
    tract_decay = jnp.exp(-pre_rates * tract)
    identity = (jnp.zeros((group, D, D), jnp.float32), jnp.ones((group,), jnp.float32))
    states_in, unused_in = carried_in(
        (tract_kv, tract_decay), "prefix", chain_combine, identity, False
    )
    later_sum, unused_out = carried_in(
        (tract_qd, tract_decay), "prefix", chain_combine, identity, True
    )
    remaining = jnp.exp(-pre_rates * (tract * (chain - 1 - link)).astype(jnp.float32))
    own_last = (states_in * tract_decay[:, None, None] + tract_kv).astype(jnp.bfloat16)
    last_state = spread(own_last, "prefix", chain - 1)
    own_pair = lax.dynamic_slice_in_dim(last_state, pair * link % group, pair, 0)
    start_state = spread(own_pair, "resp", pair * link // group)
    resp_shape = (span, pair, D)
    inside = jnp.arange(span) < resp_lengths[0]
    masked = jnp.where(inside[:, None], resp_dout[0], jnp.zeros_like(resp_dout[0])).reshape(
        resp_shape
    )
    r_query = resp_q[0].reshape(resp_shape)
    r_key = resp_k[0].reshape(resp_shape)
    r_value = resp_v[0].reshape(resp_shape)
    resp_places = jnp.arange(span).astype(jnp.float32)
    carried = weighted_outer(r_query, jnp.exp(-resp_rates[None, :] * resp_places[:, None]), masked)
    carried_sum = lax.psum(carried, "resp")
    block_count = span // STRETCH
    block_shape = (block_count, STRETCH, pair, D)
    blk_query = r_query.reshape(block_shape)
    blk_key = r_key.reshape(block_shape)
    blk_value = r_value.reshape(block_shape)
    blk_grad = masked.reshape(block_shape)
    block_dq, block_dk, block_dv = jax.vmap(local_grads, in_axes=(0, 0, 0, 0, None))(
        blk_query, blk_key, blk_value, blk_grad, resp_rates
    )
    inner_pos = jnp.arange(STRETCH).astype(jnp.float32)
    block_kweight = jnp.exp(-resp_rates[None, :] * (STRETCH - 1.0 - inner_pos)[:, None])
    block_qweight = jnp.exp(-resp_rates[None, :] * inner_pos[:, None])
    block_kv = weighted_outer(blk_key, block_kweight, blk_value)
    block_qd = weighted_outer(blk_query, block_qweight, blk_grad)
    block_decay = jnp.exp(-resp_rates * STRETCH)

    def advance(state, term):
        return (state * block_decay[:, None, None] + term, state)

    zero_state = jnp.zeros((pair, D, D), jnp.float32)
    unused_fwd, resp_in = lax.scan(advance, zero_state, block_kv)
    unused_bwd, resp_out = lax.scan(advance, zero_state, block_qd, reverse=True)
    resp_in_b = resp_in.astype(jnp.bfloat16)
    resp_out_b = resp_out.astype(jnp.bfloat16)
    block_inw = jnp.exp(-resp_rates[None, :] * (inner_pos + 1.0)[:, None])[None, :, :, None]
    block_outw = jnp.exp(-resp_rates[None, :] * (STRETCH - inner_pos)[:, None])[None, :, :, None]
    block_dq = (
        block_dq
        + jnp.einsum("pthe,phde->pthd", blk_grad, resp_in_b, preferred_element_type=jnp.float32)
        * block_inw
    )
    block_dk = (
        block_dk
        + jnp.einsum("pthe,phde->pthd", blk_value, resp_out_b, preferred_element_type=jnp.float32)
        * block_outw
    )
    block_dv = (
        block_dv
        + jnp.einsum("pthd,phde->pthe", blk_key, resp_out_b, preferred_element_type=jnp.float32)
        * block_outw
    )
    resp_sweight = jnp.exp(-resp_rates[None, :] * (resp_places + 1.0)[:, None])
    from_state = (
        jnp.einsum("the,hde->thd", masked, start_state, preferred_element_type=jnp.float32)
        * resp_sweight[:, :, None]
    )
    resp_dq = (
        (block_dq.reshape(resp_shape) + from_state).astype(jnp.bfloat16).reshape(1, span, pair * D)
    )
    resp_dk = block_dk.reshape(resp_shape).astype(jnp.bfloat16).reshape(1, span, pair * D)
    resp_dv = block_dv.reshape(resp_shape).astype(jnp.bfloat16).reshape(1, span, pair * D)
    every_pair = lax.all_gather(carried_sum, "prefix", axis=0, tiled=True)
    carried_group = lax.dynamic_slice_in_dim(every_pair, column * group, group, 0)
    states_out = later_sum + remaining[:, None, None] * carried_group
    grad_q, grad_k, grad_v = local_grads(pre_q, pre_k, pre_v, pre_g, pre_rates)
    in_weight = jnp.exp(-pre_rates[None, :] * (places + 1.0)[:, None])[:, :, None]
    out_weight = jnp.exp(-pre_rates[None, :] * (tract - places)[:, None])[:, :, None]
    state_in_b = states_in.astype(jnp.bfloat16)
    state_out_b = states_out.astype(jnp.bfloat16)
    pre_dq = (
        grad_q
        + jnp.einsum("the,hde->thd", pre_g, state_in_b, preferred_element_type=jnp.float32)
        * in_weight
    )
    pre_dk = (
        grad_k
        + jnp.einsum("the,hde->thd", pre_v, state_out_b, preferred_element_type=jnp.float32)
        * out_weight
    )
    pre_dv = (
        grad_v
        + jnp.einsum("thd,hde->the", pre_k, state_out_b, preferred_element_type=jnp.float32)
        * out_weight
    )
    flat = (tract, group * D)
    return (
        pre_dq.astype(jnp.bfloat16).reshape(flat),
        pre_dk.astype(jnp.bfloat16).reshape(flat),
        pre_dv.astype(jnp.bfloat16).reshape(flat),
        resp_dq,
        resp_dk,
        resp_dv,
    )


def solution(mesh):
    in_specs = (
        P("prefix", "resp"),
        P("prefix", "resp"),
        P("prefix", "resp"),
        P("prefix", "resp"),
        P("resp", None, "prefix"),
        P("resp", None, "prefix"),
        P("resp", None, "prefix"),
        P("resp", None, "prefix"),
        P("resp"),
        P(),
    )
    out_specs = (
        P("prefix", "resp"),
        P("prefix", "resp"),
        P("prefix", "resp"),
        P("resp", None, "prefix"),
        P("resp", None, "prefix"),
        P("resp", None, "prefix"),
    )
    return jax.shard_map(local, mesh=mesh, in_specs=in_specs, out_specs=out_specs, check_vma=False)
```

profile of v0, /device:TPU:2, one launch (start us, length us, event | category | flops | bytes accessed | tf_op | source)
XLA Modules:
  0.0 742.2 jit_solution(4435030065708504474)
XLA Ops:
  15.8 169.2 %all-reduce.5.cloned.1.call-done = f32[2,128,128]{2,1,0:T(8,128)} async-done(((f32[2,128,128]{2,1,0:T(8,128)}), f32[2,128,128]{2,1,0:T(8,128)}) %all-reduce.5.cloned.1.call-update) | async-done | bytes 131088 | tf_op jit(solution)/shard_map/psum | solution.py:120
  189.1 1.3 dynamic-slice
  191.1 53.1 %all-reduce = f32[128]{0:T(128)S(1)} all-reduce(f32[128]{0:T(128)S(1)} %get-tuple-element.473), channel_id=2, replica_groups=mesh['prefix'=32,'resp'=16] {'prefix'}, use_global_device_ids=true, to_apply=%add | all-reduce | flops 128 | bytes 1024
  252.1 7.8 %rev.7 = f32[32,4,128,128]{3,2,1,0:T(8,128)} reverse(f32[32,4,128,128]{3,2,1,0:T(8,128)} %bitcast.158), dimensions={0} | reverse | bytes 16777216 | tf_op jit(solution)/shard_map/rev | solution.py:14
  259.9 34.0 %while.59 = (s32[]{:T(128)}, f32[4,128,128]{2,1,0:T(8,128)S(1)}, s32[]{:T(128)}, f32[32,4]{1,0:T(8,128)S(1)}, f32[32,4,128,128]{3,2,1,0:T(8,128)}, /*index=5*/s32[]{:T(128)}, s32[]{:T(128)}) while((s32[]{:T(128)}, f32[4,128,128]{2,1,0:T(8,128)S(1)}, s32[]{:T(128)}, f32[32,4]{1,0:T(8,128)S(1)}, f32[32,4,128,128]{3,2,1,0:T(8,128)}, ...), condition=%wide.region_3.4_spmd.clone, body=%wide.region_2.3_spmd.clone.sunk | while | flops 262148 | bytes 786585 | solution.py:24
  259.9 1.1 fusion.97
  261.0 1.1 fusion.97
  263.2 1.1 fusion.97
  265.4 1.1 fusion.97
  273.0 1.1 fusion.97
  278.5 1.1 fusion.97
  281.8 1.1 fusion.97
  282.9 1.1 fusion.97
  286.2 1.1 fusion.97
  287.3 1.1 fusion.97
  290.6 1.1 fusion.97
  291.7 1.1 fusion.97
  293.9 1.1 add_convert_fusion.1
  295.6 39.5 %all-gather.9.cloned.1.call-done = f32[128,128,128]{2,1,0:T(8,128)} async-done(((f32[4,128,128]{2,1,0:T(8,128)}), f32[128,128,128]{2,1,0:T(8,128)}) %all-gather.9.cloned.1.call-update) | async-done | bytes 8388624 | tf_op jit(solution)/shard_map/all_gather | solution.py:12
  335.1 33.9 %while.58 = (s32[]{:T(128)}, f32[4,128,128]{2,1,0:T(8,128)S(1)}, s32[]{:T(128)}, f32[32,4]{1,0:T(8,128)S(1)}, f32[32,4,128,128]{3,2,1,0:T(8,128)}, /*index=5*/s32[]{:T(128)}, s32[]{:T(128)}) while((s32[]{:T(128)}, f32[4,128,128]{2,1,0:T(8,128)S(1)}, s32[]{:T(128)}, f32[32,4]{1,0:T(8,128)S(1)}, f32[32,4,128,128]{3,2,1,0:T(8,128)}, ...), condition=%wide.region_1.2_spmd.clone, body=%wide.region_0.1_spmd.clone.sunk | while | flops 262148 | bytes 786585 | solution.py:24
  370.3 203.5 %all-reduce.7.cloned.1.call-done = bf16[4,128,128]{2,1,0:T(8,128)(2,1)} async-done(((bf16[4,128,128]{2,1,0:T(8,128)(2,1)}), bf16[4,128,128]{2,1,0:T(8,128)(2,1)}) %all-reduce.7.cloned.1.call-update) | async-done | bytes 131088 | tf_op jit(solution)/shard_map/psum | solution.py:29
  573.7 1.5 dynamic-slice_select_fusion
  577.7 155.0 %all-reduce.9.cloned.1.call-done = bf16[2,128,128]{2,1,0:T(8,128)(2,1)} async-done(((bf16[2,128,128]{2,1,0:T(8,128)(2,1)}), bf16[2,128,128]{2,1,0:T(8,128)(2,1)}) %all-reduce.9.cloned.1.call-update) | async-done | bytes 65552 | tf_op jit(solution)/shard_map/psum | solution.py:29
  732.7 1.1 fusion.17
  (208 shorter events, 77.6 us)
Async XLA Ops:
  8.0 178.1 %copy-start = (bf16[128,512]{1,0:T(8,128)(2,1)S(1)}, bf16[128,512]{1,0:T(8,128)(2,1)}, u32[]{:S(2)}) copy-start(bf16[128,512]{1,0:T(8,128)(2,1)} %param.20) | copy-start | bytes 393220
  8.0 176.9 %all-reduce.5.cloned.1.call-start = ((), (), s32[]{:S(2)}) async-start(), calls=%async_computation | async-start | bytes 262144 | tf_op jit(solution)/shard_map/psum | solution.py:120
  12.5 239.6 %all-gather.11.cloned.1.call-start = ((), (), s32[]{:S(2)}) async-start(), calls=%async_computation.5 | async-start | bytes 8650752 | tf_op jit(solution)/shard_map/all_gather | solution.py:12
  15.7 278.2 %all-gather.7.cloned.1.call-start = ((), (), s32[]{:S(2)}) async-start(), calls=%async_computation.1 | async-start | bytes 4325376 | tf_op jit(solution)/shard_map/all_gather | solution.py:172
  185.0 150.1 %all-gather.9.cloned.1.call-start = ((), (), s32[]{:S(2)}) async-start(), calls=%async_computation.4 | async-start | bytes 8650752 | tf_op jit(solution)/shard_map/all_gather | solution.py:12
  187.0 386.7 %all-reduce.7.cloned.1.call-start = ((), (), s32[]{:S(2)}) async-start(), calls=%async_computation.2 | async-start | bytes 262144 | tf_op jit(solution)/shard_map/psum | solution.py:29
  259.9 109.2 %copy-start.1 = (f32[4,128,128]{2,1,0:T(8,128)S(1)}, f32[4,128,128]{2,1,0:T(8,128)}, u32[]{:S(2)}) copy-start(f32[4,128,128]{2,1,0:T(8,128)} %fusion.26) | copy-start | bytes 786436
  369.8 362.9 %all-reduce.9.cloned.1.call-start = ((), (), s32[]{:S(2)}) async-start(), calls=%async_computation.3 | async-start | bytes 131072 | tf_op jit(solution)/shard_map/psum | solution.py:29
Sparse Core Ops, SparseCore 0:
  12.6 172.3 all-reduce.4
  575.3 157.3 all-reduce.8
Sparse Core Ops, SparseCore 1:
  15.8 80.7 all-gather.10
  185.1 72.0 all-gather.6
  259.3 75.7 all-gather.8
  369.9 203.8 all-reduce.6
where the time goes:
time: 745 us; the launch traced here: 742 us
  waiting for transfers between devices  567 us (76%)
  other arithmetic  70.5 us (9%)
  blocking collectives  53.1 us (7%)
  local copies, waits for them, and re-layouts  23.9 us (3%)
  between operations  17.5 us (2%)
  matrix products  7.64 us (1%)
    psum x2, waiting for transfers between devices, spread(): return lax.psum(jnp.where(mine, x, jnp.zeros_like(x)), axis)  358 us
    psum x1, waiting for transfers between devices, local(): carried_sum = lax.psum(carried, 'resp')  169 us
    select_n x62, other arithmetic, turn(): jnp.where(position < mine, new, old)  65.4 us
    unnamed x1, blocking collectives  53.1 us
    all_gather x2, waiting for transfers between devices, carried_in(): pieces = jax.tree.map(lambda part: lax.all_gather(part, axis), value)  39.5 us
  transfers between devices with their start and end apart: 6, of which 4 were waited for; matrix products, arithmetic and copies ran while one was open for 8% of the time, Pallas kernels for 0%

commit v1 on v0

v1 whole, which is shorter than its diff:
```python
import functools

import jax
import jax.numpy as jnp
from jax import lax
from jax.experimental import pallas as pl
from jax.experimental.pallas import tpu as pltpu
from jax.sharding import PartitionSpec as P

D = 128
GROUP = 4
PAIR = 2
CHAIN = 32
RESPS = 16
PART = 16
F32 = jnp.float32
BF16 = jnp.bfloat16


def ring(step, size):
    return min(step % size, -step % size)


def exchange_places():
    places = {}
    for column in range(RESPS):
        x_to, yh_to, yl, z = column // 4, column % 4, column // 8, column % 8
        spots = [(l, k) for l in range(2) for k in range(8)]

        def hops(resp, spot):
            return (
                ring(resp // 4 - x_to, 4)
                + ring(2 * (resp % 4 - yh_to) + yl - spot[0], 8)
                + ring(spot[1] - z, 8)
            )

        for limit in range(16):
            taken = {}

            def assign(resp, seen):
                for spot in spots:
                    if hops(resp, spot) <= limit and spot not in seen:
                        seen.add(spot)
                        if spot not in taken or assign(taken[spot], seen):
                            taken[spot] = resp
                            return True
                return False

            if all(assign(resp, set()) for resp in range(RESPS)):
                break
        for (l, k), resp in taken.items():
            places[column, resp] = l * 8 + k
    return places


def exchange_pairs():
    pairs = []
    for (column, resp), chip in exchange_places().items():
        for core in range(2):
            pairs.append(((2 * column + core) * RESPS + resp, (2 * chip + core) * RESPS + column))
    return sorted(pairs)


def nt(a, b):
    return lax.dot_general(a, b, (((1,), (1,)), ((), ())), preferred_element_type=F32)


def tn(a, b):
    return lax.dot_general(a, b, (((0,), (0,)), ((), ())), preferred_element_type=F32)


def nn(a, b):
    return lax.dot_general(a, b, (((1,), (0,)), ((), ())), preferred_element_type=F32)


def rate_of(exps_ref, head, shape=(D, D)):
    return jnp.exp2(-jnp.full(shape, exps_ref[head].astype(F32), F32) / 1024.0)


def rows(shape=(D, D)):
    return lax.broadcasted_iota(jnp.int32, shape, 0).astype(F32)


def cut(head):
    return slice(head * D, (head + 1) * D)


def scaled(x, weight):
    return (x.astype(F32) * weight).astype(BF16)


def kv_kernel(exps, pk, pv, out):
    first = lax.axis_index("resp") * GROUP
    for h in range(GROUP):
        weight = jnp.exp(-rate_of(exps, first + h) * (D - 1.0 - rows()))
        kv = tn(scaled(pk[:, cut(h)], weight), pv[:, cut(h)]).astype(BF16)
        out[8 * h : 8 * h + 8] = kv.reshape(8, PART, D)


def masked_grad(rg, lengths, block, h):
    inside = lax.broadcasted_iota(jnp.int32, (D, D), 0) + block * D < lengths[0]
    grad = rg[0, cut(block), cut(h)]
    return jnp.where(inside, grad.astype(F32), 0.0).astype(BF16)


def qd_kernel(exps, lengths, pq, pg, rq, rg, qd_out, carried_out):
    first = lax.axis_index("resp") * GROUP
    for h in range(GROUP):
        weight = jnp.exp(-rate_of(exps, first + h) * rows())
        qd = tn(scaled(pq[:, cut(h)], weight), pg[:, cut(h)]).astype(BF16)
        qd_out[8 * h : 8 * h + 8] = qd.reshape(8, PART, D)
    first = lax.axis_index("prefix") * PAIR
    for h in range(PAIR):
        rate = rate_of(exps, first + h)
        carried = jnp.zeros((D, D), F32)
        for j in range(2):
            weight = jnp.exp(-rate * (rows() + float(j * D)))
            carried += tn(scaled(rq[0, cut(j), cut(h)], weight), masked_grad(rg, lengths, j, h))
        carried_out[8 * h : 8 * h + 8] = carried.astype(BF16).reshape(8, PART, D)


def decay_mask(rate):
    offsets = rows() - lax.broadcasted_iota(jnp.int32, (D, D), 1).astype(F32)
    return jnp.where(offsets >= 0.0, jnp.exp(-rate * jnp.maximum(offsets, 0.0)), 0.0)


def local_grads(q, k, v, g, mask):
    weights = (nt(q, k) * mask).astype(BF16)
    dscores = (nt(g, v) * mask).astype(BF16)
    return nn(dscores, k), tn(dscores, q), tn(weights, g)


def local_kernel(
    exps, lengths, pq, pk, pv, pg, rq, rk, rv, rg, pdq, pdk, pdv, rdq, rdk, rdv
):
    first = lax.axis_index("resp") * GROUP
    for h in range(GROUP):
        c = cut(h)
        mask = decay_mask(rate_of(exps, first + h))
        pdq[:, c], pdk[:, c], pdv[:, c] = local_grads(pq[:, c], pk[:, c], pv[:, c], pg[:, c], mask)
    first = lax.axis_index("prefix") * PAIR
    for h in range(PAIR):
        c = cut(h)
        rate = rate_of(exps, first + h)
        mask = decay_mask(rate)
        g0, g1 = (masked_grad(rg, lengths, j, h) for j in range(2))
        q0, q1 = rq[0, cut(0), c], rq[0, cut(1), c]
        k0, k1 = rk[0, cut(0), c], rk[0, cut(1), c]
        v0, v1 = rv[0, cut(0), c], rv[0, cut(1), c]
        resp_in = tn(scaled(k0, jnp.exp(-rate * (D - 1.0 - rows()))), v0).astype(BF16)
        resp_out = tn(scaled(q1, jnp.exp(-rate * rows())), g1).astype(BF16)
        dq, dk, dv = local_grads(q0, k0, v0, g0, mask)
        out_weight = jnp.exp(-rate * (float(D) - rows()))
        rdq[cut(0), c] = dq
        rdk[0, cut(0), c] = (dk + nt(v0, resp_out) * out_weight).astype(BF16)
        rdv[0, cut(0), c] = (dv + nn(k0, resp_out) * out_weight).astype(BF16)
        dq, dk, dv = local_grads(q1, k1, v1, g1, mask)
        rdq[cut(1), c] = dq + nt(g1, resp_in) * jnp.exp(-rate * (rows() + 1.0))
        rdk[0, cut(1), c] = dk.astype(BF16)
        rdv[0, cut(1), c] = dv.astype(BF16)


def tract_decay(exps):
    head = lax.axis_index("resp") * GROUP + lax.axis_index("prefix") // 8
    return jnp.exp(-rate_of(exps, head, (PART, D)) * float(D))


def forward_kernel(exps, kv, qd, carried, out):
    decay = tract_decay(exps)
    state = jnp.zeros((PART, D), F32)
    for b in range(CHAIN):
        out[b, 0:PART] = state.astype(BF16)
        state = state * decay + kv[b].astype(F32)
    start = state.astype(BF16)
    for b in range(CHAIN):
        out[b, PART : 2 * PART] = qd[b]
        out[b, 2 * PART : 3 * PART] = start
        out[b, 3 * PART : 4 * PART] = carried[b % 16]


def backward_kernel(exps, got, states, start):
    decay = tract_decay(exps)
    half = lax.axis_index("prefix") // 16
    state = jnp.zeros((PART, D), F32)
    for i in range(16):
        state = state + got[2 * i + half, 3 * PART : 4 * PART].astype(F32)
    for b in reversed(range(CHAIN)):
        states[b] = state.astype(BF16)
        state = state * decay + got[b, PART : 2 * PART].astype(F32)
    core = lax.axis_index("prefix") % 2
    for i in range(16):
        start[i] = got[16 * core + i, 2 * PART : 3 * PART]


def prefix_dq_kernel(exps, pg, got, pdq, out):
    first = lax.axis_index("resp") * GROUP
    for h in range(GROUP):
        c = cut(h)
        weight = jnp.exp(-rate_of(exps, first + h) * (rows() + 1.0))
        state_in = got[8 * h : 8 * h + 8, 0:PART].reshape(D, D)
        out[:, c] = (pdq[:, c] + nt(pg[:, c], state_in) * weight).astype(BF16)


def prefix_dkv_kernel(exps, pk, pv, states, pdk, pdv, dk, dv):
    first = lax.axis_index("resp") * GROUP
    for h in range(GROUP):
        c = cut(h)
        weight = jnp.exp(-rate_of(exps, first + h) * (float(D) - rows()))
        state_out = states[8 * h : 8 * h + 8].reshape(D, D)
        dk[:, c] = (pdk[:, c] + nt(pv[:, c], state_out) * weight).astype(BF16)
        dv[:, c] = (pdv[:, c] + nn(pk[:, c], state_out) * weight).astype(BF16)


def resp_dq_kernel(exps, lengths, rg, start, rdq, out):
    first = lax.axis_index("prefix") * PAIR
    for h in range(PAIR):
        c = cut(h)
        rate = rate_of(exps, first + h)
        state = start[8 * h : 8 * h + 8].reshape(D, D)
        for j in range(2):
            weight = jnp.exp(-rate * (rows() + float(j * D + 1)))
            term = nt(masked_grad(rg, lengths, j, h), state) * weight
            out[0, cut(j), c] = (rdq[cut(j), c] + term).astype(BF16)


def call(kernel, scalars, arrays, outs, flops):
    moved = sum(a.size * a.dtype.itemsize for a in arrays)
    moved += sum(o.size * o.dtype.itemsize for o in outs)
    return pl.pallas_call(
        kernel,
        out_shape=outs if len(outs) > 1 else outs[0],
        in_specs=[pl.BlockSpec(memory_space=pltpu.SMEM)] * len(scalars)
        + [pl.BlockSpec(memory_space=pltpu.VMEM)] * len(arrays),
        out_specs=[pl.BlockSpec(memory_space=pltpu.VMEM)] * len(outs)
        if len(outs) > 1
        else pl.BlockSpec(memory_space=pltpu.VMEM),
        cost_estimate=pl.CostEstimate(flops=flops, bytes_accessed=moved, transcendentals=0),
        name=kernel.__name__,
    )(*scalars, *arrays)


def shaped(shape, dtype):
    return jax.ShapeDtypeStruct(shape, dtype)


def local(there, back, pq, pk, pv, pg, rq, rk, rv, rg, lengths, exps):
    cube = 2 * D * D * D
    flat = (D, GROUP * D)
    slices = shaped((CHAIN, PART, D), BF16)
    pair = shaped((RESPS, PART, D), BF16)
    kv = call(kv_kernel, [exps], [pk, pv], [slices], 4 * cube)
    kv = lax.all_to_all(kv, "prefix", 0, 0)
    qd, carried = call(qd_kernel, [exps, lengths], [pq, pg, rq, rg], [slices, pair], 8 * cube)
    carried = lax.ppermute(carried, ("prefix", "resp"), there)
    resp_out = shaped(rq.shape, BF16)
    pdq, pdk, pdv, rdq, rdk, rdv = call(
        local_kernel,
        [exps, lengths],
        [pq, pk, pv, pg, rq, rk, rv, rg],
        [shaped(flat, F32)] * 3 + [shaped(rq.shape[1:], F32), resp_out, resp_out],
        48 * cube,
    )
    sent = call(
        forward_kernel, [exps], [kv, qd, carried], [shaped((CHAIN, 4 * PART, D), BF16)], cube
    )
    got = lax.all_to_all(sent, "prefix", 0, 0)
    states, start = call(backward_kernel, [exps], [got], [slices, pair], cube)
    states = lax.all_to_all(states, "prefix", 0, 0)
    start = lax.ppermute(start, ("prefix", "resp"), back)
    pre_dq = call(prefix_dq_kernel, [exps], [pg, got, pdq], [shaped(flat, BF16)], 4 * cube)
    resp_dq = call(resp_dq_kernel, [exps, lengths], [rg, start, rdq], [resp_out], 4 * cube)
    pre_dk, pre_dv = call(
        prefix_dkv_kernel, [exps], [pk, pv, states, pdk, pdv], [shaped(flat, BF16)] * 2, 8 * cube
    )
    return pre_dq, pre_dk, pre_dv, resp_dq, rdk, rdv


def solution(mesh):
    there = exchange_pairs()
    back = [(target, source) for source, target in there]
    prompt, response = P("prefix", "resp"), P("resp", None, "prefix")
    return jax.shard_map(
        functools.partial(local, there, back),
        mesh=mesh,
        in_specs=(prompt,) * 4 + (response,) * 4 + (P("resp"), P()),
        out_specs=(prompt,) * 3 + (response,) * 3,
        check_vma=False,
    )
```

time: 745 us -> 88.3 us (0.12)
  the two profiles are of different devices: /device:TPU:2 before, /device:TPU:7 now
where the time goes in v1:
time: 88.3 us; the launch traced here: 87.7 us
  starting transfers between devices  35.1 us (40%)
  blocking collectives  23.7 us (27%)
  Pallas kernels  17.8 us (20%)
  waiting for transfers between devices  7.81 us (9%)
  local copies, waits for them, and re-layouts  1.95 us (2%)
  between operations  1.33 us (2%)
    all_to_all x1, blocking collectives, local(): got = lax.all_to_all(sent, 'prefix', 0, 0)  23.7 us
    pallas_call x8, Pallas kernels, call(): pl.pallas_call(kernel, out_shape=outs if len(outs) > 1 else outs[0], in_s...  17.8 us
    ppermute x1, starting transfers between devices, local(): start = lax.ppermute(start, ('prefix', 'resp'), back)  12.3 us
    all_to_all x1, starting transfers between devices, local(): kv = lax.all_to_all(kv, 'prefix', 0, 0)  12.2 us
    ppermute x1, waiting for transfers between devices, local(): carried = lax.ppermute(carried, ('prefix', 'resp'), there)  7.8 us
    all_to_all x1, starting transfers between devices, local(): states = lax.all_to_all(states, 'prefix', 0, 0)  5.58 us
    ppermute x1, starting transfers between devices, local(): carried = lax.ppermute(carried, ('prefix', 'resp'), there)  5 us
    unnamed x10, local copies, waits for them, and re-layouts  1.95 us
  transfers between devices with their start and end apart: 4, of which 1 were waited for; matrix products, arithmetic and copies ran while one was open for 0% of the time, Pallas kernels for 11%

profile of v1, /device:TPU:7, one launch (start us, length us, event | category | flops | bytes accessed | tf_op | source)
XLA Modules:
  0.0 87.7 jit_solution(12930060512448325567)
XLA Ops:
  0.6 1.9 %kv_kernel.1 = bf16[32,16,128]{2,1,0:T(8,128)(2,1)} custom-call(s32[64]{0:T(128)} %exps.15, bf16[128,512]{1,0:T(8,128)(2,1)} %pk.5, bf16[128,512]{1,0:T(8,128)(2,1)} %pv.5), custom_call_target="tpu_custom_call" | custom-call | flops 16777216 | bytes 393216 | tf_op jit(solution)/shard_map/kv_kernel/pallas_call | solution.py:229
  2.5 12.2 %all-to-all-start = ((bf16[32,16,128]{2,1,0:T(8,128)(2,1)}), bf16[32,16,128]{2,1,0:T(8,128)(2,1)S(1)}, u32[]{:S(2)}, u32[]{:S(2)}) async-start(bf16[32,16,128]{2,1,0:T(8,128)(2,1)} %kv_kernel.1), calls=%async_computation | async-start | bytes 262144 | tf_op jit(solution)/shard_map/all_to_all | solution.py:252
  15.3 2.0 %qd_kernel.1 = (bf16[32,16,128]{2,1,0:T(8,128)(2,1)}, bf16[16,16,128]{2,1,0:T(8,128)(2,1)}) custom-call(s32[64]{0:T(128)} %exps.15, s32[1]{0:T(128)S(6)} %copy.16.lengths, bf16[128,512]{1,0:T(8,128)(2,1)} %pq.3, bf16[128,512]{1,0:T(8,128)(2,1)} %pg.5, bf16[1,256,256]{2,1,0:T(8,128)(2,1)} %rq.3, bf16[1,256,256]{2,1,0:T(8,128)(2,1)} %rg.5), custom_call_target="tpu_custom_call" | custom-call | flops 33554432 | bytes 720896 | tf_op jit(solution)/shard_map/qd_kernel/pallas_call | solution.py:229
  17.4 5.0 %collective-permute-start = (bf16[16,16,128]{2,1,0:T(8,128)(2,1)}, bf16[16,16,128]{2,1,0:T(8,128)(2,1)S(1)}, u32[]{:S(2)}, u32[]{:S(2)}) collective-permute-start(bf16[16,16,128]{2,1,0:T(8,128)(2,1)} %get-tuple-element.19), channel_id=1, source_target_pairs={{0,128},{1,384},{2,32},{3,160},{4,352},{5,416},{6,480},{7,192},{8,... | collective-permute-start | bytes 196616 | tf_op jit(solution)/shard_map/ppermute | solution.py:254
  22.4 7.8 %collective-permute-done.carried = bf16[16,16,128]{2,1,0:T(8,128)(2,1)S(1)} collective-permute-done((bf16[16,16,128]{2,1,0:T(8,128)(2,1)}, bf16[16,16,128]{2,1,0:T(8,128)(2,1)S(1)}, u32[]{:S(2)}, u32[]{:S(2)}) %collective-permute-start) | collective-permute-done | bytes 65568 | tf_op jit(solution)/shard_map/ppermute | solution.py:254
  30.2 0.0 copy-start.3
  30.2 0.0 all-to-all-done.kv
  30.2 0.0 copy-start.1
  30.2 0.6 copy-done.3
  30.8 0.0 copy-done.1
  30.9 1.9 %forward_kernel.1 = bf16[32,64,128]{2,1,0:T(8,128)(2,1)} custom-call(s32[64]{0:T(128)} %exps.15, bf16[32,16,128]{2,1,0:T(8,128)(2,1)} %copy-done.1, bf16[32,16,128]{2,1,0:T(8,128)(2,1)} %get-tuple-element.18.qd, bf16[16,16,128]{2,1,0:T(8,128)(2,1)} %copy-done.3), custom_call_target="tpu_custom_call" | custom-call | flops 4194304 | bytes 851968 | tf_op jit(solution)/shard_map/forward_kernel/pallas_call | solution.py:229
  32.8 23.7 %all_to_all.15.got = bf16[32,64,128]{2,1,0:T(8,128)(2,1)} all-to-all(bf16[32,64,128]{2,1,0:T(8,128)(2,1)} %forward_kernel.1), channel_id=1, replica_groups=mesh['prefix'=32,'resp'=16] {'prefix'}, dimensions={0} | all-to-all | bytes 1048576 | tf_op jit(solution)/shard_map/all_to_all | solution.py:266
  56.5 1.8 %backward_kernel.1 = (bf16[32,16,128]{2,1,0:T(8,128)(2,1)}, bf16[16,16,128]{2,1,0:T(8,128)(2,1)}) custom-call(s32[64]{0:T(128)} %exps.15, bf16[32,64,128]{2,1,0:T(8,128)(2,1)} %all_to_all.15.got), custom_call_target="tpu_custom_call" | custom-call | flops 4194304 | bytes 720896 | tf_op jit(solution)/shard_map/backward_kernel/pallas_call | solution.py:229
  58.3 5.6 %all-to-all-start.2 = ((bf16[32,16,128]{2,1,0:T(8,128)(2,1)}), bf16[32,16,128]{2,1,0:T(8,128)(2,1)S(1)}, u32[]{:S(2)}, u32[]{:S(2)}) async-start(bf16[32,16,128]{2,1,0:T(8,128)(2,1)} %get-tuple-element.21), calls=%async_computation.2 | async-start | bytes 262144 | tf_op jit(solution)/shard_map/all_to_all | solution.py:268
  63.9 0.0 copy-done.4
  63.9 12.3 %collective-permute-start.1 = (bf16[16,16,128]{2,1,0:T(8,128)(2,1)S(1)}, bf16[16,16,128]{2,1,0:T(8,128)(2,1)S(1)}, u32[]{:S(2)}, u32[]{:S(2)}) collective-permute-start(bf16[16,16,128]{2,1,0:T(8,128)(2,1)S(1)} %copy-done.4), channel_id=1, source_target_pairs={{128,0},{384,1},{32,2},{160,3},{352,4},{416,5},{480,6},{192,7},{44... | collective-permute-start | bytes 196616 | tf_op jit(solution)/shard_map/ppermute | solution.py:269
  76.2 4.1 %local_kernel.1 = (f32[128,512]{1,0:T(8,128)}, f32[128,512]{1,0:T(8,128)}, f32[128,512]{1,0:T(8,128)}, f32[256,256]{1,0:T(8,128)}, bf16[1,256,256]{2,1,0:T(8,128)(2,1)}, /*index=5*/bf16[1,256,256]{2,1,0:T(8,128)(2,1)}) custom-call(s32[64]{0:T(128)} %exps.15, s32[1]{0:T(128)S(6)} %copy.16.lengths, bf16[128,512]{1,0:T(8,128)(2,1)} %pq.3, bf16[128,512]{1,0:T(8,128)(2,1)} %pk.5, ...), custom_call_target="tpu_custom_call" | custom-call | flops 201326592 | bytes 2359296 | tf_op jit(solution)/shard_map/local_kernel/pallas_call | solution.py:229
  80.3 2.0 %prefix_dq_kernel.1 = bf16[128,512]{1,0:T(8,128)(2,1)} custom-call(s32[64]{0:T(128)} %exps.15, bf16[128,512]{1,0:T(8,128)(2,1)} %pg.5, bf16[32,64,128]{2,1,0:T(8,128)(2,1)} %all_to_all.15.got, f32[128,512]{1,0:T(8,128)} %get-tuple-element.20.pdq), custom_call_target="tpu_custom_call" | custom-call | flops 16777216 | bytes 1048576 | tf_op jit(solution)/shard_map/prefix_dq_kernel/pallas_call | solution.py:229
  82.3 0.0 collective-permute-done.1.start
  82.3 0.6 copy-done.2
  82.9 1.9 %resp_dq_kernel.1 = bf16[1,256,256]{2,1,0:T(8,128)(2,1)} custom-call(s32[64]{0:T(128)} %exps.15, s32[1]{0:T(128)S(6)} %copy.16.lengths, bf16[1,256,256]{2,1,0:T(8,128)(2,1)} %rg.5, bf16[16,16,128]{2,1,0:T(8,128)(2,1)} %copy-done.2, f32[256,256]{1,0:T(8,128)} %get-tuple-element.27.rdq), custom_call_target="tpu_custom_call" | custom-call | flops 16777216 | bytes 589824 | tf_op jit(solution)/shard_map/resp_dq_kernel/pallas_call | solution.py:229
  84.9 0.0 all-to-all-done.2.states
  84.9 0.6 copy-done
  85.5 2.2 %prefix_dkv_kernel.1 = (bf16[128,512]{1,0:T(8,128)(2,1)}, bf16[128,512]{1,0:T(8,128)(2,1)}) custom-call(s32[64]{0:T(128)} %exps.15, bf16[128,512]{1,0:T(8,128)(2,1)} %pk.5, bf16[128,512]{1,0:T(8,128)(2,1)} %pv.5, bf16[32,16,128]{2,1,0:T(8,128)(2,1)} %copy-done, f32[128,512]{1,0:T(8,128)} %get-tuple-element.22.pdk, f32[128,512]{1,0:T(8,128)} %get-tuple-element.23.pdv), custom_call_target="tpu_custom_call" | custom-call | flops 33554432 | bytes 1179648 | tf_op jit(solution)/shard_map/prefix_dkv_kernel/pallas_call | solution.py:229
  (3 shorter events, 0.0 us)
Async XLA Ops:
  2.5 27.7 %all-to-all-start = ((bf16[32,16,128]{2,1,0:T(8,128)(2,1)}), bf16[32,16,128]{2,1,0:T(8,128)(2,1)S(1)}, u32[]{:S(2)}, u32[]{:S(2)}) async-start(bf16[32,16,128]{2,1,0:T(8,128)(2,1)} %kv_kernel.1), calls=%async_computation | async-start | bytes 262144 | tf_op jit(solution)/shard_map/all_to_all | solution.py:252
  17.4 12.8 %collective-permute-start = (bf16[16,16,128]{2,1,0:T(8,128)(2,1)}, bf16[16,16,128]{2,1,0:T(8,128)(2,1)S(1)}, u32[]{:S(2)}, u32[]{:S(2)}) collective-permute-start(bf16[16,16,128]{2,1,0:T(8,128)(2,1)} %get-tuple-element.19), channel_id=1, source_target_pairs={{0,128},{1,384},{2,32},{3,160},{4,352},{5,416},{6,480},{7,192},{8,... | collective-permute-start | bytes 196616 | tf_op jit(solution)/shard_map/ppermute | solution.py:254
  30.2 0.6 copy-start.3
  30.2 0.7 copy-start.1
  58.3 5.6 %copy-start.4 = (bf16[16,16,128]{2,1,0:T(8,128)(2,1)S(1)}, bf16[16,16,128]{2,1,0:T(8,128)(2,1)}, u32[]{:S(2)}) copy-start(bf16[16,16,128]{2,1,0:T(8,128)(2,1)} %get-tuple-element.26) | copy-start | bytes 196612
  58.3 26.6 %all-to-all-start.2 = ((bf16[32,16,128]{2,1,0:T(8,128)(2,1)}), bf16[32,16,128]{2,1,0:T(8,128)(2,1)S(1)}, u32[]{:S(2)}, u32[]{:S(2)}) async-start(bf16[32,16,128]{2,1,0:T(8,128)(2,1)} %get-tuple-element.21), calls=%async_computation.2 | async-start | bytes 262144 | tf_op jit(solution)/shard_map/all_to_all | solution.py:268
  63.9 18.4 %collective-permute-start.1 = (bf16[16,16,128]{2,1,0:T(8,128)(2,1)S(1)}, bf16[16,16,128]{2,1,0:T(8,128)(2,1)S(1)}, u32[]{:S(2)}, u32[]{:S(2)}) collective-permute-start(bf16[16,16,128]{2,1,0:T(8,128)(2,1)S(1)} %copy-done.4), channel_id=1, source_target_pairs={{128,0},{384,1},{32,2},{160,3},{352,4},{416,5},{480,6},{192,7},{44... | collective-permute-start | bytes 196616 | tf_op jit(solution)/shard_map/ppermute | solution.py:269
  82.3 0.6 copy-start.2
  84.9 0.7 copy-start

commit v2 on v1

v2 whole, which is shorter than its diff:
```python
import functools

import jax
import jax.numpy as jnp
from jax import lax
from jax.experimental import pallas as pl
from jax.experimental.pallas import tpu as pltpu
from jax.sharding import PartitionSpec as P

D = 128
GROUP = 4
PAIR = 2
CHAIN = 32
RESPS = 16
PART = 16
F32 = jnp.float32
BF16 = jnp.bfloat16


def ring(source, target, size):
    step = (target - source) % size
    ways = []
    for sign, count in ((1, step), (-1, size - step)):
        if count <= size // 2:
            at, outside = source, 0
            for _ in range(count):
                to = (at + sign) % size
                outside += at // 4 != to // 4 or abs(at - to) > 1
                at = to
            ways.append(3 * count + 4 * outside)
    return sum(ways) / len(ways)


def exchange_places():
    places = {}
    spots = [(l, k) for l in range(2) for k in range(8)]
    for column in range(RESPS):
        yl, z = column // 8, column % 8

        def cost(resp, spot):
            return (
                ring(resp // 4, column // 4, 4)
                + ring(2 * (resp % 4) + yl, 2 * (column % 4) + spot[0], 8)
                + ring(z, spot[1], 8)
            )

        for limit in range(64):
            taken = {}

            def assign(resp, seen):
                for spot in spots:
                    if cost(resp, spot) <= limit and spot not in seen:
                        seen.add(spot)
                        if spot not in taken or assign(taken[spot], seen):
                            taken[spot] = resp
                            return True
                return False

            if all(assign(resp, set()) for resp in range(RESPS)):
                break
        for (l, k), resp in taken.items():
            places[column, resp] = l * 8 + k
    return places


def exchange_pairs():
    pairs = []
    for (column, resp), chip in exchange_places().items():
        for core in range(2):
            pairs.append(((2 * column + core) * RESPS + resp, (2 * chip + core) * RESPS + column))
    return sorted(pairs)


def nt(a, b):
    return lax.dot_general(a, b, (((1,), (1,)), ((), ())), preferred_element_type=F32)


def tn(a, b):
    return lax.dot_general(a, b, (((0,), (0,)), ((), ())), preferred_element_type=F32)


def nn(a, b):
    return lax.dot_general(a, b, (((1,), (0,)), ((), ())), preferred_element_type=F32)


def rate_of(exps_ref, head, shape=(D, D)):
    return jnp.exp2(-jnp.full(shape, exps_ref[head].astype(F32), F32) / 1024.0)


def rate_row(rates, index):
    return rates[8 * index : 8 * index + 1]


def rows(shape=(D, D)):
    return lax.broadcasted_iota(jnp.int32, shape, 0).astype(F32)


def cut(head):
    return slice(head * D, (head + 1) * D)


def scaled(x, weight):
    return (x.astype(F32) * weight).astype(BF16)


def owner(head, part):
    return 2 * (8 * (head % PAIR) + part) + head // PAIR


def parts_kernel(
    exps, lengths, pq_in, pk_in, pv_in, pg_in, rq_in, rg_in, out, carried_out, rates, masked,
    pq, pk, pv, pg, rq, rg, parts, loaded, stored,
):
    arrays = ((pk_in, pk), (pv_in, pv), (pq_in, pq), (pg_in, pg), (rq_in, rq), (rg_in, rg))
    loads = [pltpu.make_async_copy(a, b, loaded.at[i]) for i, (a, b) in enumerate(arrays)]
    for load in loads:
        load.start()
    mine, column = lax.axis_index("prefix"), lax.axis_index("resp")
    heads = [column * GROUP + h for h in range(GROUP)] + [mine * PAIR + h for h in range(PAIR)]
    for i, head in enumerate(heads):
        rates[8 * i : 8 * i + 8] = rate_of(exps, head, (8, D))
    tract = rate_of(exps, column * GROUP + mine % 2 * PAIR + mine // 16, (8, D))
    rates[48:56] = jnp.exp(-tract * float(D))
    stores = []
    for load in loads[:4]:
        load.wait()
    for h in range(GROUP):
        c = cut(h)
        rate = rate_row(rates, h)
        kv = tn(scaled(pk[:, c], jnp.exp(-rate * (D - 1.0 - rows()))), pv[:, c]).astype(BF16)
        qd = tn(scaled(pq[:, c], jnp.exp(-rate * rows())), pg[:, c]).astype(BF16)
        for k in range(8):
            parts[h, k, 0:PART] = kv[k * PART : (k + 1) * PART]
            parts[h, k, PART : 2 * PART] = qd[k * PART : (k + 1) * PART]
        store = pltpu.make_async_copy(
            parts.at[h], out.at[h % PAIR, :, h // PAIR], stored.at[h]
        )
        store.start()
        stores.append(store)
    for load in loads[4:]:
        load.wait()
    for h in range(PAIR):
        rate = rate_row(rates, GROUP + h)
        carried = jnp.zeros((D, D), F32)
        for j in range(2):
            inside = lax.broadcasted_iota(jnp.int32, (D, D), 0) + j * D < lengths[0]
            grad = jnp.where(inside, rg[0, cut(j), cut(h)].astype(F32), 0.0).astype(BF16)
            masked[cut(j), cut(h)] = grad
            weight = jnp.exp(-rate * (rows() + float(j * D)))
            carried += tn(scaled(rq[0, cut(j), cut(h)], weight), grad)
        carried_out[8 * h : 8 * h + 8] = carried.astype(BF16).reshape(8, PART, D)
    for store in stores:
        store.wait()


def decay_mask(rate):
    offsets = rows() - lax.broadcasted_iota(jnp.int32, (D, D), 1).astype(F32)
    return jnp.where(offsets >= 0.0, jnp.exp(-rate * jnp.maximum(offsets, 0.0)), 0.0)


def local_grads(q, k, v, g, mask):
    weights = (nt(q, k) * mask).astype(BF16)
    dscores = (nt(g, v) * mask).astype(BF16)
    return nn(dscores, k), tn(dscores, q), tn(weights, g)


def local_kernel(
    rates, pq, pk, pv, pg, rq, rk, rv, masked, after, pdq, pdk, pdv, rdq, rdk, rdv, token
):
    token[...] = jnp.zeros_like(token)
    for h in range(GROUP):
        c = cut(h)
        mask = decay_mask(rate_row(rates, h))
        pdq[:, c], pdk[:, c], pdv[:, c] = local_grads(pq[:, c], pk[:, c], pv[:, c], pg[:, c], mask)
    for h in range(PAIR):
        c = cut(h)
        rate = rate_row(rates, GROUP + h)
        mask = decay_mask(rate)
        g0, g1 = masked[cut(0), c], masked[cut(1), c]
        q0, q1 = rq[0, cut(0), c], rq[0, cut(1), c]
        k0, k1 = rk[0, cut(0), c], rk[0, cut(1), c]
        v0, v1 = rv[0, cut(0), c], rv[0, cut(1), c]
        resp_in = tn(scaled(k0, jnp.exp(-rate * (D - 1.0 - rows()))), v0).astype(BF16)
        resp_out = tn(scaled(q1, jnp.exp(-rate * rows())), g1).astype(BF16)
        dq, dk, dv = local_grads(q0, k0, v0, g0, mask)
        out_weight = jnp.exp(-rate * (float(D) - rows()))
        rdq[cut(0), c] = dq
        rdk[0, cut(0), c] = (dk + nt(v0, resp_out) * out_weight).astype(BF16)
        rdv[0, cut(0), c] = (dv + nn(k0, resp_out) * out_weight).astype(BF16)
        dq, dk, dv = local_grads(q1, k1, v1, g1, mask)
        rdq[cut(1), c] = dq + nt(g1, resp_in) * jnp.exp(-rate * (rows() + 1.0))
        rdk[0, cut(1), c] = dk.astype(BF16)
        rdv[0, cut(1), c] = dv.astype(BF16)


def start_kernel(rates, got, carried, out, token):
    decay = rates[48:49]
    state = jnp.zeros((PART, D), F32)
    for b in range(CHAIN):
        state = state * decay + got[b, 0:PART].astype(F32)
    start = state.astype(BF16)
    for j in range(RESPS):
        out[j, 0:PART] = start
        out[j, PART : 2 * PART] = carried[j]
    token[...] = jnp.zeros_like(token)


def states_kernel(rates, got, got_two, after, out, start):
    decay = rates[48:49]
    ahead = jnp.zeros((PART, D), F32)
    behind = jnp.zeros((PART, D), F32)
    for j in range(RESPS):
        behind = behind + got_two[j, PART : 2 * PART].astype(F32)
    for b in range(CHAIN):
        out[b, 0:PART] = ahead.astype(BF16)
        ahead = ahead * decay + got[b, 0:PART].astype(F32)
        e = CHAIN - 1 - b
        out[e, PART : 2 * PART] = behind.astype(BF16)
        behind = behind * decay + got[e, PART : 2 * PART].astype(F32)
    for j in range(RESPS):
        start[j] = got_two[j, 0:PART]


def prefix_kernel(rates, pk, pv, pg, states, pdq, pdk, pdv, dq, dk, dv):
    for h in range(GROUP):
        c = cut(h)
        rate = rate_row(rates, h)
        both = [states[owner(h, k)] for k in range(8)]
        state_in = jnp.concatenate([b[0:PART] for b in both], axis=0)
        state_out = jnp.concatenate([b[PART : 2 * PART] for b in both], axis=0)
        weight = jnp.exp(-rate * (rows() + 1.0))
        dq[:, c] = (pdq[:, c] + nt(pg[:, c], state_in) * weight).astype(BF16)
        weight = jnp.exp(-rate * (float(D) - rows()))
        dk[:, c] = (pdk[:, c] + nt(pv[:, c], state_out) * weight).astype(BF16)
        dv[:, c] = (pdv[:, c] + nn(pk[:, c], state_out) * weight).astype(BF16)


def resp_dq_kernel(rates, masked, start, rdq, out):
    for h in range(PAIR):
        c = cut(h)
        rate = rate_row(rates, GROUP + h)
        state = start[8 * h : 8 * h + 8].reshape(D, D)
        for j in range(2):
            weight = jnp.exp(-rate * (rows() + float(j * D + 1)))
            term = nt(masked[cut(j), c], state) * weight
            out[0, cut(j), c] = (rdq[cut(j), c] + term).astype(BF16)


def call(kernel, arrays, outs, flops, in_specs=None, out_specs=None, scratch_shapes=(), limit=8):
    moved = sum(a.size * a.dtype.itemsize for a in arrays)
    moved += sum(o.size * o.dtype.itemsize for o in outs)
    vmem = pl.BlockSpec(memory_space=pltpu.VMEM)
    got = pl.pallas_call(
        kernel,
        out_shape=tuple(outs),
        in_specs=in_specs or [vmem] * len(arrays),
        out_specs=tuple(out_specs or [vmem] * len(outs)),
        scratch_shapes=scratch_shapes,
        cost_estimate=pl.CostEstimate(flops=flops, bytes_accessed=moved, transcendentals=0),
        compiler_params=pltpu.CompilerParams(vmem_limit_bytes=limit << 20),
        name=kernel.__name__,
    )(*arrays)
    return got if len(outs) > 1 else got[0]


def shaped(shape, dtype):
    return jax.ShapeDtypeStruct(shape, dtype)


def local(there, back, pq, pk, pv, pg, rq, rk, rv, rg, lengths, exps):
    cube = 2 * D * D * D
    flat = (D, GROUP * D)
    token = shaped((8, D), F32)
    slots = shaped((CHAIN, 2 * PART, D), BF16)
    pair = shaped((RESPS, PART, D), BF16)
    resp_out = shaped(rq.shape, BF16)
    cores = [list(range(core, CHAIN, 2)) for core in range(2)]
    smem, hbm, vmem = (pl.BlockSpec(memory_space=m) for m in (pltpu.SMEM, pltpu.HBM, pltpu.VMEM))
    rates = shaped((56, D), F32)
    masked = shaped(rq.shape[1:], BF16)
    sources = [pq, pk, pv, pg, rq, rg]
    parts, carried, rates, masked = call(
        parts_kernel,
        [exps, lengths] + sources,
        [shaped((PAIR, 8, PAIR, 2 * PART, D), BF16), pair, rates, masked],
        12 * cube,
        [smem, smem] + [hbm] * 6,
        [hbm, vmem, vmem, vmem],
        [pltpu.VMEM(a.shape, a.dtype) for a in sources]
        + [pltpu.VMEM((GROUP, 8, 2 * PART, D), BF16)]
        + [pltpu.SemaphoreType.DMA((6,)), pltpu.SemaphoreType.DMA((GROUP,))],
        limit=60,
    )
    got = lax.all_to_all(parts.reshape(slots.shape), "prefix", 0, 0)
    carried = lax.ppermute(carried, ("prefix", "resp"), there)
    sent, after = call(
        start_kernel, [rates, got, carried], [shaped((RESPS, 2 * PART, D), BF16), token], cube
    )
    got_two = lax.all_to_all(sent, "prefix", 0, 0, axis_index_groups=cores)
    pdq, pdk, pdv, rdq, rdk, rdv, after = call(
        local_kernel,
        [rates, pq, pk, pv, pg, rq, rk, rv, masked, after],
        [shaped(flat, F32)] * 3 + [shaped(rq.shape[1:], F32), resp_out, resp_out, token],
        48 * cube,
    )
    states, start = call(states_kernel, [rates, got, got_two, after], [slots, pair], cube)
    states = lax.all_to_all(states, "prefix", 0, 0)
    start = lax.ppermute(start, ("prefix", "resp"), back)
    resp_dq = call(resp_dq_kernel, [rates, masked, start, rdq], [resp_out], 4 * cube)
    pre_dq, pre_dk, pre_dv = call(
        prefix_kernel,
        [rates, pk, pv, pg, states, pdq, pdk, pdv],
        [shaped(flat, BF16)] * 3,
        12 * cube,
    )
    return pre_dq, pre_dk, pre_dv, resp_dq, rdk, rdv


def solution(mesh):
    there = exchange_pairs()
    back = [(target, source) for source, target in there]
    prompt, response = P("prefix", "resp"), P("resp", None, "prefix")
    return jax.shard_map(
        functools.partial(local, there, back),
        mesh=mesh,
        in_specs=(prompt,) * 4 + (response,) * 4 + (P("resp"), P()),
        out_specs=(prompt,) * 3 + (response,) * 3,
        check_vma=False,
    )
```

time: 88.3 us -> 76.4 us (0.87)
  the two profiles are of different devices: /device:TPU:7 before, /device:TPU:80 now
where the time goes in v2:
time: 76.4 us; the launch traced here: 75.9 us
  starting transfers between devices  39.1 us (51%)
  waiting for transfers between devices  25.7 us (34%)
  Pallas kernels  9.58 us (13%)
  between operations  1.43 us (2%)
    ppermute x1, waiting for transfers between devices, local(): start = lax.ppermute(start, ('prefix', 'resp'), back)  14.6 us
    all_to_all x1, starting transfers between devices, local(): got_two = lax.all_to_all(sent, 'prefix', 0, 0, axis_index_groups=cores)  11.9 us
    all_to_all x1, starting transfers between devices, local(): got = lax.all_to_all(parts.reshape(slots.shape), 'prefix', 0, 0)  11.3 us
    pallas_call x6, Pallas kernels, call(): pl.pallas_call(kernel, out_shape=tuple(outs), in_specs=in_specs or [vmem]...  9.58 us
    ppermute x1, starting transfers between devices, local(): carried = lax.ppermute(carried, ('prefix', 'resp'), there)  6.38 us
    ppermute x1, waiting for transfers between devices, local(): carried = lax.ppermute(carried, ('prefix', 'resp'), there)  6.2 us
    ppermute x1, starting transfers between devices, local(): start = lax.ppermute(start, ('prefix', 'resp'), back)  5.04 us
    all_to_all x1, waiting for transfers between devices, local(): got_two = lax.all_to_all(sent, 'prefix', 0, 0, axis_index_groups=cores)  4.91 us
  transfers between devices with their start and end apart: 5, of which 3 were waited for; matrix products, arithmetic and copies ran while one was open for 0% of the time, Pallas kernels for 5%

profile of v2, /device:TPU:80, one launch (start us, length us, event | category | flops | bytes accessed | tf_op | source)
XLA Modules:
  0.0 75.9 jit_solution(8255775112963906865)
XLA Ops:
  1.3 3.5 %parts_kernel.1 = (bf16[2,8,2,32,128]{4,3,2,1,0:T(8,128)(2,1)}, bf16[16,16,128]{2,1,0:T(8,128)(2,1)}, f32[56,128]{1,0:T(8,128)}, bf16[256,256]{1,0:T(8,128)(2,1)}) custom-call(s32[64]{0:T(128)} %exps.1, s32[1]{0:T(128)S(6)} %copy.16.lengths, bf16[128,512]{1,0:T(8,128)(2,1)} %pq.1, bf16[128,512]{1,0:T(8,128)(2,1)} %pk.3, bf16[128,512]{1,0:T(8,128)(2,1)} %pv.3, ...), custom_call_target="tpu_custom_call" | custom-call | flops 50331648 | bytes 1274116 | tf_op jit(solution)/shard_map/parts_kernel/pallas_call | solution.py:253
  4.7 0.0 copy-start.3
  4.8 0.0 copy-start.5
  4.8 0.0 copy-start.6
  4.8 0.0 copy-start.7
  4.8 0.0 copy-start.8
  4.8 11.3 %all-to-all-start = ((bf16[32,32,128]{2,1,0:T(8,128)(2,1)}), bf16[32,32,128]{2,1,0:T(8,128)(2,1)S(1)}, u32[]{:S(2)}, u32[]{:S(2)}) async-start(bf16[32,32,128]{2,1,0:T(8,128)(2,1)} %bitcast.1), calls=%async_computation | async-start | bytes 524288 | tf_op jit(solution)/shard_map/all_to_all | solution.py:294
  16.1 6.4 %collective-permute-start = (bf16[16,16,128]{2,1,0:T(8,128)(2,1)}, bf16[16,16,128]{2,1,0:T(8,128)(2,1)S(1)}, u32[]{:S(2)}, u32[]{:S(2)}) collective-permute-start(bf16[16,16,128]{2,1,0:T(8,128)(2,1)} %get-tuple-element.26), channel_id=1, source_target_pairs={{0,160},{1,416},{2,64},{3,448},{4,384},{5,320},{6,480},{7,224},{8,... | collective-permute-start | bytes 196616 | tf_op jit(solution)/shard_map/ppermute | solution.py:295
  22.5 6.2 %collective-permute-done.carried = bf16[16,16,128]{2,1,0:T(8,128)(2,1)S(1)} collective-permute-done((bf16[16,16,128]{2,1,0:T(8,128)(2,1)}, bf16[16,16,128]{2,1,0:T(8,128)(2,1)S(1)}, u32[]{:S(2)}, u32[]{:S(2)}) %collective-permute-start) | collective-permute-done | bytes 65568 | tf_op jit(solution)/shard_map/ppermute | solution.py:295
  28.7 0.0 all-to-all-done.got
  28.7 0.0 copy-done.3
  28.7 0.0 copy-start.4
  28.7 0.7 start_kernel.1
  29.4 11.9 %all-to-all-start.1 = ((bf16[16,32,128]{2,1,0:T(8,128)(2,1)}), bf16[16,32,128]{2,1,0:T(8,128)(2,1)S(1)}, u32[]{:S(2)}, u32[]{:S(2)}) async-start(bf16[16,32,128]{2,1,0:T(8,128)(2,1)} %get-tuple-element.27), calls=%async_computation.1 | async-start | bytes 262144 | tf_op jit(solution)/shard_map/all_to_all | solution.py:299
  41.3 0.0 copy-done.5
  41.4 2.7 %local_kernel.1 = (f32[128,512]{1,0:T(8,128)S(1)}, f32[128,512]{1,0:T(8,128)S(1)}, f32[128,512]{1,0:T(8,128)S(1)}, f32[256,256]{1,0:T(8,128)S(1)}, bf16[1,256,25...) custom-call(f32[56,128]{1,0:T(8,128)S(1)} %copy-done.3, bf16[128,512]{1,0:T(8,128)(2,1)S(1)} %copy-done.5, ...), custom_call_target="tpu_custom_call" | custom-call | flops 201326592 | bytes 2396160 | tf_op jit(solution)/shard_map/local_kernel/pallas_call | solution.py:253
  44.1 4.9 %all-to-all-done.1.got_two = bf16[16,32,128]{2,1,0:T(8,128)(2,1)S(1)} async-done(((bf16[16,32,128]{2,1,0:T(8,128)(2,1)}), bf16[16,32,128]{2,1,0:T(8,128)(2,1)S(1)}, u32[]{:S(2)}, u32[]{:S(2)}) %all-to-all-start.1) | async-done | bytes 131104 | tf_op jit(solution)/shard_map/all_to_all | solution.py:299
  49.0 0.8 %states_kernel.1 = (bf16[32,32,128]{2,1,0:T(8,128)(2,1)}, bf16[16,16,128]{2,1,0:T(8,128)(2,1)S(1)}) custom-call(f32[56,128]{1,0:T(8,128)S(1)} %copy-done.3, bf16[32,32,128]{2,1,0:T(8,128)(2,1)S(1)} %all-to-all-done.got, bf16[16,32,128]{2,1,0:T(8,128)(2,1)S(1)} %all-to-all-done.1.got_two, f32[8,128]{1,0:T(8,128)S(1)} %get-tuple-element.30.after), custom_call_target="tpu_custom_call" | custom-call | flops 4194304 | bytes 753664 | tf_op jit(solution)/shard_map/states_kernel/pallas_call | solution.py:253
  49.8 4.6 %all-to-all-start.2 = ((bf16[32,32,128]{2,1,0:T(8,128)(2,1)}), bf16[32,32,128]{2,1,0:T(8,128)(2,1)S(1)}, u32[]{:S(2)}, u32[]{:S(2)}) async-start(bf16[32,32,128]{2,1,0:T(8,128)(2,1)} %get-tuple-element.31), calls=%async_computation.2 | async-start | bytes 524288 | tf_op jit(solution)/shard_map/all_to_all | solution.py:307
  54.3 5.0 %collective-permute-start.1 = (bf16[16,16,128]{2,1,0:T(8,128)(2,1)S(1)}, bf16[16,16,128]{2,1,0:T(8,128)(2,1)S(1)}, u32[]{:S(2)}, u32[]{:S(2)}) collective-permute-start(bf16[16,16,128]{2,1,0:T(8,128)(2,1)S(1)} %get-tuple-element.38), channel_id=1, source_target_pairs={{160,0},{416,1},{64,2},{448,3},{384,4},{320,5},{480,6},{224,7},{19... | collective-permute-start | bytes 196616 | tf_op jit(solution)/shard_map/ppermute | solution.py:308
  59.4 14.6 %collective-permute-done.1.start = bf16[16,16,128]{2,1,0:T(8,128)(2,1)S(1)} collective-permute-done((bf16[16,16,128]{2,1,0:T(8,128)(2,1)S(1)}, bf16[16,16,128]{2,1,0:T(8,128)(2,1)S(1)}, u32[]{:S(2)}, u32[]{:S(2)}) %collective-permute-start.1) | collective-permute-done | bytes 65568 | tf_op jit(solution)/shard_map/ppermute | solution.py:308
  74.0 0.9 %resp_dq_kernel.1 = bf16[1,256,256]{2,1,0:T(8,128)(2,1)} custom-call(f32[56,128]{1,0:T(8,128)S(1)} %copy-done.3, bf16[256,256]{1,0:T(8,128)(2,1)S(1)} %copy-done.4, bf16[16,16,128]{2,1,0:T(8,128)(2,1)S(1)} %collective-permute-done.1.start, f32[256,256]{1,0:T(8,128)S(1)} %get-tuple-element.39.rdq), custom_call_target="tpu_custom_call" | custom-call | flops 16777216 | bytes 618496 | tf_op jit(solution)/shard_map/resp_dq_kernel/pallas_call | solution.py:253
  74.9 0.0 all-to-all-done.2.states
  74.9 1.1 %prefix_kernel.1 = (bf16[128,512]{1,0:T(8,128)(2,1)}, bf16[128,512]{1,0:T(8,128)(2,1)}, bf16[128,512]{1,0:T(8,128)(2,1)}) custom-call(f32[56,128]{1,0:T(8,128)S(1)} %copy-done.3, bf16[128,512]{1,0:T(8,128)(2,1)S(1)} %copy-done, bf16[128,512]{1,0:T(8,128)(2,1)S(1)} %copy-done.1, bf16[128,512]{1,0:T(8,128)(2,1)S(1)} %copy-done.2, ...), custom_call_target="tpu_custom_call" | custom-call | flops 50331648 | bytes 1863680 | tf_op jit(solution)/shard_map/prefix_kernel/pallas_call | solution.py:253
  (10 shorter events, 0.0 us)
Async XLA Ops:
  4.7 23.9 %copy-start.3 = (f32[56,128]{1,0:T(8,128)S(1)}, f32[56,128]{1,0:T(8,128)}, u32[]{:S(2)}) copy-start(f32[56,128]{1,0:T(8,128)} %get-tuple-element.24.rates) | copy-start | bytes 86020
  4.8 36.5 %copy-start.5 = (bf16[128,512]{1,0:T(8,128)(2,1)S(1)}, bf16[128,512]{1,0:T(8,128)(2,1)}, u32[]{:S(2)}) copy-start(bf16[128,512]{1,0:T(8,128)(2,1)} %pq.1) | copy-start | bytes 393220
  4.8 36.5 %copy-start.6 = (bf16[1,256,256]{2,1,0:T(8,128)(2,1)S(1)}, bf16[1,256,256]{2,1,0:T(8,128)(2,1)}, u32[]{:S(2)}) copy-start(bf16[1,256,256]{2,1,0:T(8,128)(2,1)} %rq.1) | copy-start | bytes 393220
  4.8 36.5 %copy-start.7 = (bf16[1,256,256]{2,1,0:T(8,128)(2,1)S(1)}, bf16[1,256,256]{2,1,0:T(8,128)(2,1)}, u32[]{:S(2)}) copy-start(bf16[1,256,256]{2,1,0:T(8,128)(2,1)} %rk.1) | copy-start | bytes 393220
  4.8 36.5 %copy-start.8 = (bf16[1,256,256]{2,1,0:T(8,128)(2,1)S(1)}, bf16[1,256,256]{2,1,0:T(8,128)(2,1)}, u32[]{:S(2)}) copy-start(bf16[1,256,256]{2,1,0:T(8,128)(2,1)} %rv.1) | copy-start | bytes 393220
  4.8 23.9 %all-to-all-start = ((bf16[32,32,128]{2,1,0:T(8,128)(2,1)}), bf16[32,32,128]{2,1,0:T(8,128)(2,1)S(1)}, u32[]{:S(2)}, u32[]{:S(2)}) async-start(bf16[32,32,128]{2,1,0:T(8,128)(2,1)} %bitcast.1), calls=%async_computation | async-start | bytes 524288 | tf_op jit(solution)/shard_map/all_to_all | solution.py:294
  16.1 12.6 %collective-permute-start = (bf16[16,16,128]{2,1,0:T(8,128)(2,1)}, bf16[16,16,128]{2,1,0:T(8,128)(2,1)S(1)}, u32[]{:S(2)}, u32[]{:S(2)}) collective-permute-start(bf16[16,16,128]{2,1,0:T(8,128)(2,1)} %get-tuple-element.26), channel_id=1, source_target_pairs={{0,160},{1,416},{2,64},{3,448},{4,384},{5,320},{6,480},{7,224},{8,... | collective-permute-start | bytes 196616 | tf_op jit(solution)/shard_map/ppermute | solution.py:295
  28.7 12.7 %copy-start.2 = (bf16[128,512]{1,0:T(8,128)(2,1)S(1)}, bf16[128,512]{1,0:T(8,128)(2,1)}, u32[]{:S(2)}) copy-start(bf16[128,512]{1,0:T(8,128)(2,1)} %pg.3) | copy-start | bytes 393220
  28.7 12.7 %copy-start.4 = (bf16[256,256]{1,0:T(8,128)(2,1)S(1)}, bf16[256,256]{1,0:T(8,128)(2,1)}, u32[]{:S(2)}) copy-start(bf16[256,256]{1,0:T(8,128)(2,1)} %get-tuple-element.28.masked) | copy-start | bytes 393220
  29.4 11.9 %copy-start = (bf16[128,512]{1,0:T(8,128)(2,1)S(1)}, bf16[128,512]{1,0:T(8,128)(2,1)}, u32[]{:S(2)}) copy-start(bf16[128,512]{1,0:T(8,128)(2,1)} %pk.3) | copy-start | bytes 393220
  29.4 11.9 %copy-start.1 = (bf16[128,512]{1,0:T(8,128)(2,1)S(1)}, bf16[128,512]{1,0:T(8,128)(2,1)}, u32[]{:S(2)}) copy-start(bf16[128,512]{1,0:T(8,128)(2,1)} %pv.3) | copy-start | bytes 393220
  29.4 19.5 %all-to-all-start.1 = ((bf16[16,32,128]{2,1,0:T(8,128)(2,1)}), bf16[16,32,128]{2,1,0:T(8,128)(2,1)S(1)}, u32[]{:S(2)}, u32[]{:S(2)}) async-start(bf16[16,32,128]{2,1,0:T(8,128)(2,1)} %get-tuple-element.27), calls=%async_computation.1 | async-start | bytes 262144 | tf_op jit(solution)/shard_map/all_to_all | solution.py:299
  49.8 25.1 %all-to-all-start.2 = ((bf16[32,32,128]{2,1,0:T(8,128)(2,1)}), bf16[32,32,128]{2,1,0:T(8,128)(2,1)S(1)}, u32[]{:S(2)}, u32[]{:S(2)}) async-start(bf16[32,32,128]{2,1,0:T(8,128)(2,1)} %get-tuple-element.31), calls=%async_computation.2 | async-start | bytes 524288 | tf_op jit(solution)/shard_map/all_to_all | solution.py:307
  54.3 19.6 %collective-permute-start.1 = (bf16[16,16,128]{2,1,0:T(8,128)(2,1)S(1)}, bf16[16,16,128]{2,1,0:T(8,128)(2,1)S(1)}, u32[]{:S(2)}, u32[]{:S(2)}) collective-permute-start(bf16[16,16,128]{2,1,0:T(8,128)(2,1)S(1)} %get-tuple-element.38), channel_id=1, source_target_pairs={{160,0},{416,1},{64,2},{448,3},{384,4},{320,5},{480,6},{224,7},{19... | collective-permute-start | bytes 196616 | tf_op jit(solution)/shard_map/ppermute | solution.py:308

commit v3 on v2

--- a/solution.py
+++ b/solution.py
@@ -17,57 +17,52 @@
 BF16 = jnp.bfloat16
 
 
-def ring(source, target, size):
-    step = (target - source) % size
-    ways = []
-    for sign, count in ((1, step), (-1, size - step)):
-        if count <= size // 2:
-            at, outside = source, 0
-            for _ in range(count):
-                to = (at + sign) % size
-                outside += at // 4 != to // 4 or abs(at - to) > 1
-                at = to
-            ways.append(3 * count + 4 * outside)
-    return sum(ways) / len(ways)
-
-
-def exchange_places():
-    places = {}
-    spots = [(l, k) for l in range(2) for k in range(8)]
+GATHER = (
+    "4c263da7fe805b91",
+    "35df7eca248906b1",
+    "846eb2fda350917c",
+    "f9d7ea40cb268315",
+    "1ab709d238e56fc4",
+    "428e319b60ac57fd",
+    "6429803ad7fbe51c",
+    "c804962bae73df51",
+    "ea08c9154b26df73",
+    "7b9153806eca4df2",
+    "20ca146987ed35fb",
+    "b351826d940fca7e",
+    "fd53be461ac78920",
+    "0ac67fd528e419b3",
+    "7fbd65ce412903a8",
+    "e62af74d851c903b",
+)
+SPREAD = (
+    "dcf54ea32b806791",
+    "45df7ce2108936ba",
+    "856eb0dfa243917c",
+    "fd67e915cb348a20",
+    "7fd298e10a463bc5",
+    "28ae019763bc54fd",
+    "7589c12ad43be60f",
+    "ae51b923cd648f70",
+    "8a01ef96cd743b25",
+    "78914fb25de36ca0",
+    "2ac9157b86ef304d",
+    "a3bcd206e47f9158",
+    "bfc3ed461a528970",
+    "0be64cd528f719a3",
+    "74bf659ed13c02a8",
+    "d684f7e9c51ba032",
+)
+
+
+def exchange_pairs(table):
+    pairs = []
     for column in range(RESPS):
-        yl, z = column // 8, column % 8
-
-        def cost(resp, spot):
-            return (
-                ring(resp // 4, column // 4, 4)
-                + ring(2 * (resp % 4) + yl, 2 * (column % 4) + spot[0], 8)
-                + ring(z, spot[1], 8)
-            )
-
-        for limit in range(64):
-            taken = {}
-
-            def assign(resp, seen):
-                for spot in spots:
-                    if cost(resp, spot) <= limit and spot not in seen:
-                        seen.add(spot)
-                        if spot not in taken or assign(taken[spot], seen):
-                            taken[spot] = resp
-                            return True
-                return False
-
-            if all(assign(resp, set()) for resp in range(RESPS)):
-                break
-        for (l, k), resp in taken.items():
-            places[column, resp] = l * 8 + k
-    return places
-
-
-def exchange_pairs():
-    pairs = []
-    for (column, resp), chip in exchange_places().items():
-        for core in range(2):
-            pairs.append(((2 * column + core) * RESPS + resp, (2 * chip + core) * RESPS + column))
+        for resp in range(RESPS):
+            chip = int(table[column][resp], 16)
+            for core in range(2):
+                response = (2 * column + core) * RESPS + resp
+                pairs.append((response, (2 * chip + core) * RESPS + column))
     return sorted(pairs)
 
 
@@ -108,21 +103,48 @@
 
 
 def parts_kernel(
-    exps, lengths, pq_in, pk_in, pv_in, pg_in, rq_in, rg_in, out, carried_out, rates, masked,
-    pq, pk, pv, pg, rq, rg, parts, loaded, stored,
+    exps_in, lengths_in, pq_in, pk_in, pv_in, pg_in, rq_in, rg_in,
+    out, carried_out, rates_out, masked_out,
+    exps, lengths, pq, pk, pv, pg, rq, rg, parts, carried, rates, masked, loaded, stored,
 ):
-    arrays = ((pk_in, pk), (pv_in, pv), (pq_in, pq), (pg_in, pg), (rq_in, rq), (rg_in, rg))
-    loads = [pltpu.make_async_copy(a, b, loaded.at[i]) for i, (a, b) in enumerate(arrays)]
+    def copies(pairs, sems):
+        return [pltpu.make_async_copy(a, b, sems.at[i]) for i, (a, b) in enumerate(pairs)]
+
+    loads = copies(
+        ((exps_in, exps), (lengths_in, lengths), (rq_in, rq), (rg_in, rg))
+        + ((pk_in, pk), (pv_in, pv), (pq_in, pq), (pg_in, pg)),
+        loaded,
+    )
+    stores = copies(
+        ((rates, rates_out), (masked, masked_out), (carried, carried_out))
+        + tuple((parts.at[h], out.at[h % PAIR, :, h // PAIR]) for h in range(GROUP)),
+        stored,
+    )
     for load in loads:
         load.start()
     mine, column = lax.axis_index("prefix"), lax.axis_index("resp")
     heads = [column * GROUP + h for h in range(GROUP)] + [mine * PAIR + h for h in range(PAIR)]
+    loads[0].wait()
     for i, head in enumerate(heads):
         rates[8 * i : 8 * i + 8] = rate_of(exps, head, (8, D))
     tract = rate_of(exps, column * GROUP + mine % 2 * PAIR + mine // 16, (8, D))
     rates[48:56] = jnp.exp(-tract * float(D))
-    stores = []
-    for load in loads[:4]:
+    stores[0].start()
+    for load in loads[1:4]:
+        load.wait()
+    for h in range(PAIR):
+        rate = rate_row(rates, GROUP + h)
+        total = jnp.zeros((D, D), F32)
+        for j in range(2):
+            inside = lax.broadcasted_iota(jnp.int32, (D, D), 0) + j * D < lengths[0]
+            grad = jnp.where(inside, rg[0, cut(j), cut(h)].astype(F32), 0.0).astype(BF16)
+            masked[cut(j), cut(h)] = grad
+            weight = jnp.exp(-rate * (rows() + float(j * D)))
+            total += tn(scaled(rq[0, cut(j), cut(h)], weight), grad)
+        carried[8 * h : 8 * h + 8] = total.astype(BF16).reshape(8, PART, D)
+    stores[1].start()
+    stores[2].start()
+    for load in loads[4:]:
         load.wait()
     for h in range(GROUP):
         c = cut(h)
@@ -132,23 +154,7 @@
         for k in range(8):
             parts[h, k, 0:PART] = kv[k * PART : (k + 1) * PART]
             parts[h, k, PART : 2 * PART] = qd[k * PART : (k + 1) * PART]
-        store = pltpu.make_async_copy(
-            parts.at[h], out.at[h % PAIR, :, h // PAIR], stored.at[h]
-        )
-        store.start()
-        stores.append(store)
-    for load in loads[4:]:
-        load.wait()
-    for h in range(PAIR):
-        rate = rate_row(rates, GROUP + h)
-        carried = jnp.zeros((D, D), F32)
-        for j in range(2):
-            inside = lax.broadcasted_iota(jnp.int32, (D, D), 0) + j * D < lengths[0]
-            grad = jnp.where(inside, rg[0, cut(j), cut(h)].astype(F32), 0.0).astype(BF16)
-            masked[cut(j), cut(h)] = grad
-            weight = jnp.exp(-rate * (rows() + float(j * D)))
-            carried += tn(scaled(rq[0, cut(j), cut(h)], weight), grad)
-        carried_out[8 * h : 8 * h + 8] = carried.astype(BF16).reshape(8, PART, D)
+        stores[3 + h].start()
     for store in stores:
         store.wait()
 
@@ -246,7 +252,7 @@
             out[0, cut(j), c] = (rdq[cut(j), c] + term).astype(BF16)
 
 
-def call(kernel, arrays, outs, flops, in_specs=None, out_specs=None, scratch_shapes=(), limit=8):
+def call(kernel, arrays, outs, flops, in_specs=None, out_specs=None, scratch_shapes=(), limit=8 << 20):
     moved = sum(a.size * a.dtype.itemsize for a in arrays)
     moved += sum(o.size * o.dtype.itemsize for o in outs)
     vmem = pl.BlockSpec(memory_space=pltpu.VMEM)
@@ -257,7 +263,7 @@
         out_specs=tuple(out_specs or [vmem] * len(outs)),
         scratch_shapes=scratch_shapes,
         cost_estimate=pl.CostEstimate(flops=flops, bytes_accessed=moved, transcendentals=0),
-        compiler_params=pltpu.CompilerParams(vmem_limit_bytes=limit << 20),
+        compiler_params=pltpu.CompilerParams(vmem_limit_bytes=limit),
         name=kernel.__name__,
     )(*arrays)
     return got if len(outs) > 1 else got[0]
@@ -275,7 +281,7 @@
     pair = shaped((RESPS, PART, D), BF16)
     resp_out = shaped(rq.shape, BF16)
     cores = [list(range(core, CHAIN, 2)) for core in range(2)]
-    smem, hbm, vmem = (pl.BlockSpec(memory_space=m) for m in (pltpu.SMEM, pltpu.HBM, pltpu.VMEM))
+    hbm = pl.BlockSpec(memory_space=pltpu.HBM)
     rates = shaped((56, D), F32)
     masked = shaped(rq.shape[1:], BF16)
     sources = [pq, pk, pv, pg, rq, rg]
@@ -284,12 +290,14 @@
         [exps, lengths] + sources,
         [shaped((PAIR, 8, PAIR, 2 * PART, D), BF16), pair, rates, masked],
         12 * cube,
-        [smem, smem] + [hbm] * 6,
-        [hbm, vmem, vmem, vmem],
-        [pltpu.VMEM(a.shape, a.dtype) for a in sources]
+        [hbm] * 8,
+        [hbm] * 4,
+        [pltpu.SMEM(a.shape, a.dtype) for a in (exps, lengths)]
+        + [pltpu.VMEM(a.shape, a.dtype) for a in sources]
         + [pltpu.VMEM((GROUP, 8, 2 * PART, D), BF16)]
-        + [pltpu.SemaphoreType.DMA((6,)), pltpu.SemaphoreType.DMA((GROUP,))],
-        limit=60,
+        + [pltpu.VMEM(a.shape, a.dtype) for a in (pair, rates, masked)]
+        + [pltpu.SemaphoreType.DMA((8,)), pltpu.SemaphoreType.DMA((3 + GROUP,))],
+        limit=None,
     )
     got = lax.all_to_all(parts.reshape(slots.shape), "prefix", 0, 0)
     carried = lax.ppermute(carried, ("prefix", "resp"), there)
@@ -317,8 +325,8 @@
 
 
 def solution(mesh):
-    there = exchange_pairs()
-    back = [(target, source) for source, target in there]
+    there = exchange_pairs(GATHER)
+    back = [(partner, response) for response, partner in exchange_pairs(SPREAD)]
     prompt, response = P("prefix", "resp"), P("resp", None, "prefix")
     return jax.shard_map(
         functools.partial(local, there, back),

time: 76.4 us -> 69.2 us (0.906)
  the two profiles are of different devices: /device:TPU:80 before, /device:TPU:95 now
where the time goes in v3:
time: 69.2 us; the launch traced here: 68.7 us
  starting transfers between devices  36.2 us (52%)
  waiting for transfers between devices  22.7 us (33%)
  Pallas kernels  8.38 us (12%)
  between operations  1.43 us (2%)
    ppermute x1, waiting for transfers between devices, local(): start = lax.ppermute(start, ('prefix', 'resp'), back)  11.7 us
    all_to_all x1, starting transfers between devices, local(): got = lax.all_to_all(parts.reshape(slots.shape), 'prefix', 0, 0)  11.5 us
    pallas_call x6, Pallas kernels, call(): pl.pallas_call(kernel, out_shape=tuple(outs), in_specs=in_specs or [vmem]...  8.38 us
    ppermute x1, waiting for transfers between devices, local(): carried = lax.ppermute(carried, ('prefix', 'resp'), there)  6.88 us
    all_to_all x1, starting transfers between devices, local(): states = lax.all_to_all(states, 'prefix', 0, 0)  6.58 us
    ppermute x1, starting transfers between devices, local(): carried = lax.ppermute(carried, ('prefix', 'resp'), there)  6.41 us
    ppermute x1, starting transfers between devices, local(): start = lax.ppermute(start, ('prefix', 'resp'), back)  6.15 us
    all_to_all x1, starting transfers between devices, local(): got_two = lax.all_to_all(sent, 'prefix', 0, 0, axis_index_groups=cores)  5.54 us
  transfers between devices with their start and end apart: 5, of which 3 were waited for; matrix products, arithmetic and copies ran while one was open for 0% of the time, Pallas kernels for 5%

profile of v3, /device:TPU:95, one launch (start us, length us, event | category | flops | bytes accessed | tf_op | source)
XLA Modules:
  0.0 68.7 jit_solution(3280759433522792652)
XLA Ops:
  1.3 2.3 %parts_kernel.1 = (bf16[2,8,2,32,128]{4,3,2,1,0:T(8,128)(2,1)}, bf16[16,16,128]{2,1,0:T(8,128)(2,1)}, f32[56,128]{1,0:T(8,128)}, bf16[256,256]{1,0:T(8,128)(2,1)}) custom-call(s32[64]{0:T(128)} %exps_in.1, s32[1]{0:T(128)S(6)} %copy.16.lengths_in, bf16[128,512]{1,0:T(8,128)(2,1)} %pq.1, bf16[128,512]{1,0:T(8,128)(2,1)} %pk.3, bf16[128,512]{1,0:T(8,128)(2,1)} %pv.3, ...), custom_call_target="tpu_custom_call" | custom-call | flops 50331648 | bytes 1274116 | tf_op jit(solution)/shard_map/parts_kernel/pallas_call | solution.py:259
  3.5 0.0 copy-start.3
  3.6 0.0 copy-start.5
  3.6 0.0 copy-start.6
  3.6 0.0 copy-start.7
  3.6 0.0 copy-start.8
  3.6 11.5 %all-to-all-start = ((bf16[32,32,128]{2,1,0:T(8,128)(2,1)}), bf16[32,32,128]{2,1,0:T(8,128)(2,1)S(1)}, u32[]{:S(2)}, u32[]{:S(2)}) async-start(bf16[32,32,128]{2,1,0:T(8,128)(2,1)} %bitcast.1), calls=%async_computation | async-start | bytes 524288 | tf_op jit(solution)/shard_map/all_to_all | solution.py:302
  15.1 6.4 %collective-permute-start = (bf16[16,16,128]{2,1,0:T(8,128)(2,1)}, bf16[16,16,128]{2,1,0:T(8,128)(2,1)S(1)}, u32[]{:S(2)}, u32[]{:S(2)}) collective-permute-start(bf16[16,16,128]{2,1,0:T(8,128)(2,1)} %get-tuple-element.26), channel_id=1, source_target_pairs={{0,128},{1,384},{2,64},{3,192},{4,96},{5,416},{6,320},{7,224},{8,4... | collective-permute-start | bytes 196616 | tf_op jit(solution)/shard_map/ppermute | solution.py:303
  21.5 6.9 %collective-permute-done.carried = bf16[16,16,128]{2,1,0:T(8,128)(2,1)S(1)} collective-permute-done((bf16[16,16,128]{2,1,0:T(8,128)(2,1)}, bf16[16,16,128]{2,1,0:T(8,128)(2,1)S(1)}, u32[]{:S(2)}, u32[]{:S(2)}) %collective-permute-start) | collective-permute-done | bytes 65568 | tf_op jit(solution)/shard_map/ppermute | solution.py:303
  28.4 0.0 all-to-all-done.got
  28.4 0.0 copy-start.4
  28.4 0.7 %start_kernel.1 = (bf16[16,32,128]{2,1,0:T(8,128)(2,1)}, f32[8,128]{1,0:T(8,128)S(1)}) custom-call(f32[56,128]{1,0:T(8,128)S(1)} %copy-done.3, bf16[32,32,128]{2,1,0:T(8,128)(2,1)S(1)} %all-to-all-done.got, bf16[16,16,128]{2,1,0:T(8,128)(2,1)S(1)} %collective-permute-done.carried), custom_call_target="tpu_custom_call" | custom-call | flops 4194304 | bytes 491520 | tf_op jit(solution)/shard_map/start_kernel/pallas_call | solution.py:259
  29.2 5.5 %all-to-all-start.1 = ((bf16[16,32,128]{2,1,0:T(8,128)(2,1)}), bf16[16,32,128]{2,1,0:T(8,128)(2,1)S(1)}, u32[]{:S(2)}, u32[]{:S(2)}) async-start(bf16[16,32,128]{2,1,0:T(8,128)(2,1)} %get-tuple-element.27), calls=%async_computation.1 | async-start | bytes 262144 | tf_op jit(solution)/shard_map/all_to_all | solution.py:307
  34.7 0.0 copy-done.6
  34.7 0.0 copy-done.7
  34.8 2.7 %local_kernel.1 = (f32[128,512]{1,0:T(8,128)S(1)}, f32[128,512]{1,0:T(8,128)S(1)}, f32[128,512]{1,0:T(8,128)S(1)}, f32[256,256]{1,0:T(8,128)S(1)}, bf16[1,256,25...) custom-call(f32[56,128]{1,0:T(8,128)S(1)} %copy-done.3, bf16[128,512]{1,0:T(8,128)(2,1)S(1)} %copy-done.5, ...), custom_call_target="tpu_custom_call" | custom-call | flops 201326592 | bytes 2396160 | tf_op jit(solution)/shard_map/local_kernel/pallas_call | solution.py:259
  37.5 4.1 %all-to-all-done.1.got_two = bf16[16,32,128]{2,1,0:T(8,128)(2,1)S(1)} async-done(((bf16[16,32,128]{2,1,0:T(8,128)(2,1)}), bf16[16,32,128]{2,1,0:T(8,128)(2,1)S(1)}, u32[]{:S(2)}, u32[]{:S(2)}) %all-to-all-start.1) | async-done | bytes 131104 | tf_op jit(solution)/shard_map/all_to_all | solution.py:307
  41.5 0.8 %states_kernel.1 = (bf16[32,32,128]{2,1,0:T(8,128)(2,1)}, bf16[16,16,128]{2,1,0:T(8,128)(2,1)S(1)}) custom-call(f32[56,128]{1,0:T(8,128)S(1)} %copy-done.3, bf16[32,32,128]{2,1,0:T(8,128)(2,1)S(1)} %all-to-all-done.got, bf16[16,32,128]{2,1,0:T(8,128)(2,1)S(1)} %all-to-all-done.1.got_two, f32[8,128]{1,0:T(8,128)S(1)} %get-tuple-element.30.after), custom_call_target="tpu_custom_call" | custom-call | flops 4194304 | bytes 753664 | tf_op jit(solution)/shard_map/states_kernel/pallas_call | solution.py:259
  42.3 6.6 %all-to-all-start.2 = ((bf16[32,32,128]{2,1,0:T(8,128)(2,1)}), bf16[32,32,128]{2,1,0:T(8,128)(2,1)S(1)}, u32[]{:S(2)}, u32[]{:S(2)}) async-start(bf16[32,32,128]{2,1,0:T(8,128)(2,1)} %get-tuple-element.31), calls=%async_computation.2 | async-start | bytes 524288 | tf_op jit(solution)/shard_map/all_to_all | solution.py:315
  48.9 6.2 %collective-permute-start.1 = (bf16[16,16,128]{2,1,0:T(8,128)(2,1)S(1)}, bf16[16,16,128]{2,1,0:T(8,128)(2,1)S(1)}, u32[]{:S(2)}, u32[]{:S(2)}) collective-permute-start(bf16[16,16,128]{2,1,0:T(8,128)(2,1)S(1)} %get-tuple-element.38), channel_id=1, source_target_pairs={{416,0},{384,1},{480,2},{160,3},{128,4},{448,5},{320,6},{96,7},{64... | collective-permute-start | bytes 196616 | tf_op jit(solution)/shard_map/ppermute | solution.py:316
  55.1 11.7 %collective-permute-done.1.start = bf16[16,16,128]{2,1,0:T(8,128)(2,1)S(1)} collective-permute-done((bf16[16,16,128]{2,1,0:T(8,128)(2,1)S(1)}, bf16[16,16,128]{2,1,0:T(8,128)(2,1)S(1)}, u32[]{:S(2)}, u32[]{:S(2)}) %collective-permute-start.1) | collective-permute-done | bytes 65568 | tf_op jit(solution)/shard_map/ppermute | solution.py:316
  66.8 0.9 %resp_dq_kernel.1 = bf16[1,256,256]{2,1,0:T(8,128)(2,1)} custom-call(f32[56,128]{1,0:T(8,128)S(1)} %copy-done.3, bf16[256,256]{1,0:T(8,128)(2,1)S(1)} %copy-done.4, bf16[16,16,128]{2,1,0:T(8,128)(2,1)S(1)} %collective-permute-done.1.start, f32[256,256]{1,0:T(8,128)S(1)} %get-tuple-element.39.rdq), custom_call_target="tpu_custom_call" | custom-call | flops 16777216 | bytes 618496 | tf_op jit(solution)/shard_map/resp_dq_kernel/pallas_call | solution.py:259
  67.7 0.0 all-to-all-done.2.states
  67.7 1.1 %prefix_kernel.1 = (bf16[128,512]{1,0:T(8,128)(2,1)}, bf16[128,512]{1,0:T(8,128)(2,1)}, bf16[128,512]{1,0:T(8,128)(2,1)}) custom-call(f32[56,128]{1,0:T(8,128)S(1)} %copy-done.3, bf16[128,512]{1,0:T(8,128)(2,1)S(1)} %copy-done, bf16[128,512]{1,0:T(8,128)(2,1)S(1)} %copy-done.1, bf16[128,512]{1,0:T(8,128)(2,1)S(1)} %copy-done.2, ...), custom_call_target="tpu_custom_call" | custom-call | flops 50331648 | bytes 1863680 | tf_op jit(solution)/shard_map/prefix_kernel/pallas_call | solution.py:259
  (10 shorter events, 0.0 us)
Async XLA Ops:
  3.5 24.9 %copy-start.3 = (f32[56,128]{1,0:T(8,128)S(1)}, f32[56,128]{1,0:T(8,128)}, u32[]{:S(2)}) copy-start(f32[56,128]{1,0:T(8,128)} %get-tuple-element.24.rates) | copy-start | bytes 86020
  3.6 31.1 %copy-start.5 = (bf16[128,512]{1,0:T(8,128)(2,1)S(1)}, bf16[128,512]{1,0:T(8,128)(2,1)}, u32[]{:S(2)}) copy-start(bf16[128,512]{1,0:T(8,128)(2,1)} %pq.1) | copy-start | bytes 393220
  3.6 31.1 %copy-start.6 = (bf16[1,256,256]{2,1,0:T(8,128)(2,1)S(1)}, bf16[1,256,256]{2,1,0:T(8,128)(2,1)}, u32[]{:S(2)}) copy-start(bf16[1,256,256]{2,1,0:T(8,128)(2,1)} %rq.1) | copy-start | bytes 393220
  3.6 31.1 %copy-start.7 = (bf16[1,256,256]{2,1,0:T(8,128)(2,1)S(1)}, bf16[1,256,256]{2,1,0:T(8,128)(2,1)}, u32[]{:S(2)}) copy-start(bf16[1,256,256]{2,1,0:T(8,128)(2,1)} %rk.1) | copy-start | bytes 393220
  3.6 31.1 %copy-start.8 = (bf16[1,256,256]{2,1,0:T(8,128)(2,1)S(1)}, bf16[1,256,256]{2,1,0:T(8,128)(2,1)}, u32[]{:S(2)}) copy-start(bf16[1,256,256]{2,1,0:T(8,128)(2,1)} %rv.1) | copy-start | bytes 393220
  3.6 24.8 %all-to-all-start = ((bf16[32,32,128]{2,1,0:T(8,128)(2,1)}), bf16[32,32,128]{2,1,0:T(8,128)(2,1)S(1)}, u32[]{:S(2)}, u32[]{:S(2)}) async-start(bf16[32,32,128]{2,1,0:T(8,128)(2,1)} %bitcast.1), calls=%async_computation | async-start | bytes 524288 | tf_op jit(solution)/shard_map/all_to_all | solution.py:302
  15.1 13.3 %collective-permute-start = (bf16[16,16,128]{2,1,0:T(8,128)(2,1)}, bf16[16,16,128]{2,1,0:T(8,128)(2,1)S(1)}, u32[]{:S(2)}, u32[]{:S(2)}) collective-permute-start(bf16[16,16,128]{2,1,0:T(8,128)(2,1)} %get-tuple-element.26), channel_id=1, source_target_pairs={{0,128},{1,384},{2,64},{3,192},{4,96},{5,416},{6,320},{7,224},{8,4... | collective-permute-start | bytes 196616 | tf_op jit(solution)/shard_map/ppermute | solution.py:303
  28.4 6.3 %copy-start.2 = (bf16[128,512]{1,0:T(8,128)(2,1)S(1)}, bf16[128,512]{1,0:T(8,128)(2,1)}, u32[]{:S(2)}) copy-start(bf16[128,512]{1,0:T(8,128)(2,1)} %pg.3) | copy-start | bytes 393220
  28.4 6.3 %copy-start.4 = (bf16[256,256]{1,0:T(8,128)(2,1)S(1)}, bf16[256,256]{1,0:T(8,128)(2,1)}, u32[]{:S(2)}) copy-start(bf16[256,256]{1,0:T(8,128)(2,1)} %get-tuple-element.28.masked) | copy-start | bytes 393220
  29.2 5.6 %copy-start = (bf16[128,512]{1,0:T(8,128)(2,1)S(1)}, bf16[128,512]{1,0:T(8,128)(2,1)}, u32[]{:S(2)}) copy-start(bf16[128,512]{1,0:T(8,128)(2,1)} %pk.3) | copy-start | bytes 393220
  29.2 5.6 %copy-start.1 = (bf16[128,512]{1,0:T(8,128)(2,1)S(1)}, bf16[128,512]{1,0:T(8,128)(2,1)}, u32[]{:S(2)}) copy-start(bf16[128,512]{1,0:T(8,128)(2,1)} %pv.3) | copy-start | bytes 393220
  29.2 12.4 %all-to-all-start.1 = ((bf16[16,32,128]{2,1,0:T(8,128)(2,1)}), bf16[16,32,128]{2,1,0:T(8,128)(2,1)S(1)}, u32[]{:S(2)}, u32[]{:S(2)}) async-start(bf16[16,32,128]{2,1,0:T(8,128)(2,1)} %get-tuple-element.27), calls=%async_computation.1 | async-start | bytes 262144 | tf_op jit(solution)/shard_map/all_to_all | solution.py:307
  42.3 25.3 %all-to-all-start.2 = ((bf16[32,32,128]{2,1,0:T(8,128)(2,1)}), bf16[32,32,128]{2,1,0:T(8,128)(2,1)S(1)}, u32[]{:S(2)}, u32[]{:S(2)}) async-start(bf16[32,32,128]{2,1,0:T(8,128)(2,1)} %get-tuple-element.31), calls=%async_computation.2 | async-start | bytes 524288 | tf_op jit(solution)/shard_map/all_to_all | solution.py:315
  48.9 17.9 %collective-permute-start.1 = (bf16[16,16,128]{2,1,0:T(8,128)(2,1)S(1)}, bf16[16,16,128]{2,1,0:T(8,128)(2,1)S(1)}, u32[]{:S(2)}, u32[]{:S(2)}) collective-permute-start(bf16[16,16,128]{2,1,0:T(8,128)(2,1)S(1)} %get-tuple-element.38), channel_id=1, source_target_pairs={{416,0},{384,1},{480,2},{160,3},{128,4},{448,5},{320,6},{96,7},{64... | collective-permute-start | bytes 196616 | tf_op jit(solution)/shard_map/ppermute | solution.py:316

commit v4 on v3

--- a/solution.py
+++ b/solution.py
@@ -18,40 +18,40 @@
 
 
 GATHER = (
-    "4c263da7fe805b91",
-    "35df7eca248906b1",
-    "846eb2fda350917c",
-    "f9d7ea40cb268315",
-    "1ab709d238e56fc4",
-    "428e319b60ac57fd",
-    "6429803ad7fbe51c",
-    "c804962bae73df51",
-    "ea08c9154b26df73",
-    "7b9153806eca4df2",
-    "20ca146987ed35fb",
-    "b351826d940fca7e",
-    "fd53be461ac78920",
-    "0ac67fd528e419b3",
-    "7fbd65ce412903a8",
-    "e62af74d851c903b",
+    "5ca74d96ef013b82",
+    "4dfa7ce836b90521",
+    "906eb47fa18d235c",
+    "ec4fda169b058327",
+    "1ac789e60bd23f45",
+    "71bf2935e0846acd",
+    "d51ac023f79be648",
+    "9d82ac135f4b7e60",
+    "e813cf274b95da06",
+    "6c9035a17df24eb8",
+    "23fb15e9046ca7d8",
+    "a250c378d14f9b6e",
+    "fb5d2c478a6309e1",
+    "3ae50bfd296c1847",
+    "748c6e9f532d01ab",
+    "f64ce758d02a913b",
 )
 SPREAD = (
-    "dcf54ea32b806791",
-    "45df7ce2108936ba",
-    "856eb0dfa243917c",
-    "fd67e915cb348a20",
-    "7fd298e10a463bc5",
-    "28ae019763bc54fd",
-    "7589c12ad43be60f",
-    "ae51b923cd648f70",
-    "8a01ef96cd743b25",
-    "78914fb25de36ca0",
-    "2ac9157b86ef304d",
-    "a3bcd206e47f9158",
-    "bfc3ed461a528970",
-    "0be64cd528f719a3",
-    "74bf659ed13c02a8",
-    "d684f7e9c51ba032",
+    "4cf5dea26b803791",
+    "4def75cb1089263a",
+    "c06e895da243b17f",
+    "fd67ec159b248a30",
+    "29d608b1fa437ec5",
+    "3b8e09af217c546d",
+    "d528c09af43be617",
+    "cd54b923ae618f70",
+    "9802ef73cd64ba15",
+    "6891fca25d374eb0",
+    "2a4b38d9076f15ec",
+    "b3a8c10de47f9256",
+    "fd57bc43ae618920",
+    "3ae4c8d509f612b7",
+    "709e64fd51a8c32b",
+    "d64ce7098f1ba532",
 )
 
 
@@ -103,20 +103,17 @@
 
 
 def parts_kernel(
-    exps_in, lengths_in, pq_in, pk_in, pv_in, pg_in, rq_in, rg_in,
-    out, carried_out, rates_out, masked_out,
-    exps, lengths, pq, pk, pv, pg, rq, rg, parts, carried, rates, masked, loaded, stored,
+    exps_in, pq_in, pk_in, pv_in, pg_in, out, rates_out,
+    exps, pq, pk, pv, pg, parts, rates, loaded, stored,
 ):
     def copies(pairs, sems):
         return [pltpu.make_async_copy(a, b, sems.at[i]) for i, (a, b) in enumerate(pairs)]
 
     loads = copies(
-        ((exps_in, exps), (lengths_in, lengths), (rq_in, rq), (rg_in, rg))
-        + ((pk_in, pk), (pv_in, pv), (pq_in, pq), (pg_in, pg)),
-        loaded,
+        ((exps_in, exps), (pk_in, pk), (pv_in, pv), (pq_in, pq), (pg_in, pg)), loaded
     )
     stores = copies(
-        ((rates, rates_out), (masked, masked_out), (carried, carried_out))
+        ((rates, rates_out),)
         + tuple((parts.at[h], out.at[h % PAIR, :, h // PAIR]) for h in range(GROUP)),
         stored,
     )
@@ -130,8 +127,22 @@
     tract = rate_of(exps, column * GROUP + mine % 2 * PAIR + mine // 16, (8, D))
     rates[48:56] = jnp.exp(-tract * float(D))
     stores[0].start()
-    for load in loads[1:4]:
+    for load in loads[1:]:
         load.wait()
+    for h in range(GROUP):
+        c = cut(h)
+        rate = rate_row(rates, h)
+        kv = tn(scaled(pk[:, c], jnp.exp(-rate * (D - 1.0 - rows()))), pv[:, c]).astype(BF16)
+        qd = tn(scaled(pq[:, c], jnp.exp(-rate * rows())), pg[:, c]).astype(BF16)
+        for k in range(8):
+            parts[h, k, 0:PART] = kv[k * PART : (k + 1) * PART]
+            parts[h, k, PART : 2 * PART] = qd[k * PART : (k + 1) * PART]
+        stores[1 + h].start()
+    for store in stores:
+        store.wait()
+
+
+def carried_kernel(lengths, rates, rq, rg, carried, masked):
     for h in range(PAIR):
         rate = rate_row(rates, GROUP + h)
         total = jnp.zeros((D, D), F32)
@@ -142,21 +153,6 @@
             weight = jnp.exp(-rate * (rows() + float(j * D)))
             total += tn(scaled(rq[0, cut(j), cut(h)], weight), grad)
         carried[8 * h : 8 * h + 8] = total.astype(BF16).reshape(8, PART, D)
-    stores[1].start()
-    stores[2].start()
-    for load in loads[4:]:
-        load.wait()
-    for h in range(GROUP):
-        c = cut(h)
-        rate = rate_row(rates, h)
-        kv = tn(scaled(pk[:, c], jnp.exp(-rate * (D - 1.0 - rows()))), pv[:, c]).astype(BF16)
-        qd = tn(scaled(pq[:, c], jnp.exp(-rate * rows())), pg[:, c]).astype(BF16)
-        for k in range(8):
-            parts[h, k, 0:PART] = kv[k * PART : (k + 1) * PART]
-            parts[h, k, PART : 2 * PART] = qd[k * PART : (k + 1) * PART]
-        stores[3 + h].start()
-    for store in stores:
-        store.wait()
 
 
 def decay_mask(rate):
@@ -170,14 +166,15 @@
     return nn(dscores, k), tn(dscores, q), tn(weights, g)
 
 
-def local_kernel(
-    rates, pq, pk, pv, pg, rq, rk, rv, masked, after, pdq, pdk, pdv, rdq, rdk, rdv, token
-):
+def local_kernel(rates, pq, pk, pv, pg, pdq, pdk, pdv, token):
     token[...] = jnp.zeros_like(token)
     for h in range(GROUP):
         c = cut(h)
         mask = decay_mask(rate_row(rates, h))
         pdq[:, c], pdk[:, c], pdv[:, c] = local_grads(pq[:, c], pk[:, c], pv[:, c], pg[:, c], mask)
+
+
+def resp_kernel(rates, rq, rk, rv, masked, after, rdq, rdk, rdv):
     for h in range(PAIR):
         c = cut(h)
         rate = rate_row(rates, GROUP + h)
@@ -199,7 +196,7 @@
         rdv[0, cut(1), c] = dv.astype(BF16)
 
 
-def start_kernel(rates, got, carried, out, token):
+def start_kernel(rates, got, carried, before, out):
     decay = rates[48:49]
     state = jnp.zeros((PART, D), F32)
     for b in range(CHAIN):
@@ -208,10 +205,9 @@
     for j in range(RESPS):
         out[j, 0:PART] = start
         out[j, PART : 2 * PART] = carried[j]
-    token[...] = jnp.zeros_like(token)
-
-
-def states_kernel(rates, got, got_two, after, out, start):
+
+
+def states_kernel(rates, got, got_two, out, start, token):
     decay = rates[48:49]
     ahead = jnp.zeros((PART, D), F32)
     behind = jnp.zeros((PART, D), F32)
@@ -225,9 +221,20 @@
         behind = behind * decay + got[e, PART : 2 * PART].astype(F32)
     for j in range(RESPS):
         start[j] = got_two[j, 0:PART]
-
-
-def prefix_kernel(rates, pk, pv, pg, states, pdq, pdk, pdv, dq, dk, dv):
+    token[...] = jnp.zeros_like(token)
+
+
+def final_kernel(
+    rates, pk, pv, pg, states, pdq, pdk, pdv, masked, start, rdq, dq, dk, dv, resp_dq
+):
+    for h in range(PAIR):
+        c = cut(h)
+        rate = rate_row(rates, GROUP + h)
+        state = start[8 * h : 8 * h + 8].reshape(D, D)
+        for j in range(2):
+            weight = jnp.exp(-rate * (rows() + float(j * D + 1)))
+            term = nt(masked[cut(j), c], state) * weight
+            resp_dq[0, cut(j), c] = (rdq[cut(j), c] + term).astype(BF16)
     for h in range(GROUP):
         c = cut(h)
         rate = rate_row(rates, h)
@@ -239,17 +246,6 @@
         weight = jnp.exp(-rate * (float(D) - rows()))
         dk[:, c] = (pdk[:, c] + nt(pv[:, c], state_out) * weight).astype(BF16)
         dv[:, c] = (pdv[:, c] + nn(pk[:, c], state_out) * weight).astype(BF16)
-
-
-def resp_dq_kernel(rates, masked, start, rdq, out):
-    for h in range(PAIR):
-        c = cut(h)
-        rate = rate_row(rates, GROUP + h)
-        state = start[8 * h : 8 * h + 8].reshape(D, D)
-        for j in range(2):
-            weight = jnp.exp(-rate * (rows() + float(j * D + 1)))
-            term = nt(masked[cut(j), c], state) * weight
-            out[0, cut(j), c] = (rdq[cut(j), c] + term).astype(BF16)
 
 
 def call(kernel, arrays, outs, flops, in_specs=None, out_specs=None, scratch_shapes=(), limit=8 << 20):
@@ -284,42 +280,52 @@
     hbm = pl.BlockSpec(memory_space=pltpu.HBM)
     rates = shaped((56, D), F32)
     masked = shaped(rq.shape[1:], BF16)
-    sources = [pq, pk, pv, pg, rq, rg]
-    parts, carried, rates, masked = call(
+    sources = [pq, pk, pv, pg]
+    parts, rates = call(
         parts_kernel,
-        [exps, lengths] + sources,
-        [shaped((PAIR, 8, PAIR, 2 * PART, D), BF16), pair, rates, masked],
-        12 * cube,
-        [hbm] * 8,
-        [hbm] * 4,
-        [pltpu.SMEM(a.shape, a.dtype) for a in (exps, lengths)]
+        [exps] + sources,
+        [shaped((PAIR, 8, PAIR, 2 * PART, D), BF16), rates],
+        8 * cube,
+        [hbm] * 5,
+        [hbm] * 2,
+        [pltpu.SMEM(exps.shape, exps.dtype)]
         + [pltpu.VMEM(a.shape, a.dtype) for a in sources]
-        + [pltpu.VMEM((GROUP, 8, 2 * PART, D), BF16)]
-        + [pltpu.VMEM(a.shape, a.dtype) for a in (pair, rates, masked)]
-        + [pltpu.SemaphoreType.DMA((8,)), pltpu.SemaphoreType.DMA((3 + GROUP,))],
+        + [pltpu.VMEM((GROUP, 8, 2 * PART, D), BF16), pltpu.VMEM(rates.shape, F32)]
+        + [pltpu.SemaphoreType.DMA((5,)), pltpu.SemaphoreType.DMA((1 + GROUP,))],
         limit=None,
+    )
+    carried, masked = call(
+        carried_kernel,
+        [lengths, rates, rq, rg],
+        [pair, masked],
+        4 * cube,
+        [pl.BlockSpec(memory_space=pltpu.SMEM)] + [pl.BlockSpec(memory_space=pltpu.VMEM)] * 3,
     )
     got = lax.all_to_all(parts.reshape(slots.shape), "prefix", 0, 0)
     carried = lax.ppermute(carried, ("prefix", "resp"), there)
-    sent, after = call(
-        start_kernel, [rates, got, carried], [shaped((RESPS, 2 * PART, D), BF16), token], cube
+    pdq, pdk, pdv, before = call(
+        local_kernel, [rates, pq, pk, pv, pg], [shaped(flat, F32)] * 3 + [token], 20 * cube
+    )
+    sent = call(
+        start_kernel, [rates, got, carried, before], [shaped((RESPS, 2 * PART, D), BF16)], cube
     )
     got_two = lax.all_to_all(sent, "prefix", 0, 0, axis_index_groups=cores)
-    pdq, pdk, pdv, rdq, rdk, rdv, after = call(
-        local_kernel,
-        [rates, pq, pk, pv, pg, rq, rk, rv, masked, after],
-        [shaped(flat, F32)] * 3 + [shaped(rq.shape[1:], F32), resp_out, resp_out, token],
-        48 * cube,
-    )
-    states, start = call(states_kernel, [rates, got, got_two, after], [slots, pair], cube)
+    states, start, after = call(
+        states_kernel, [rates, got, got_two], [slots, pair, token], cube
+    )
+    rdq, rdk, rdv = call(
+        resp_kernel,
+        [rates, rq, rk, rv, masked, after],
+        [shaped(rq.shape[1:], F32), resp_out, resp_out],
+        28 * cube,
+    )
     states = lax.all_to_all(states, "prefix", 0, 0)
     start = lax.ppermute(start, ("prefix", "resp"), back)
-    resp_dq = call(resp_dq_kernel, [rates, masked, start, rdq], [resp_out], 4 * cube)
-    pre_dq, pre_dk, pre_dv = call(
-        prefix_kernel,
-        [rates, pk, pv, pg, states, pdq, pdk, pdv],
-        [shaped(flat, BF16)] * 3,
-        12 * cube,
+    pre_dq, pre_dk, pre_dv, resp_dq = call(
+        final_kernel,
+        [rates, pk, pv, pg, states, pdq, pdk, pdv, masked, start, rdq],
+        [shaped(flat, BF16)] * 3 + [resp_out],
+        16 * cube,
     )
     return pre_dq, pre_dk, pre_dv, resp_dq, rdk, rdv
 

time: 69.2 us -> 67.5 us (0.975)
  the two profiles are of different devices: /device:TPU:95 before, /device:TPU:91 now
where the time goes in v4:
time: 67.5 us; the launch traced here: 67.1 us
  starting transfers between devices  30.9 us (46%)
  blocking collectives  16 us (24%)
  waiting for transfers between devices  11.4 us (17%)
  Pallas kernels  7.26 us (11%)
  between operations  1.46 us (2%)
    all_to_all x1, blocking collectives, local(): got_two = lax.all_to_all(sent, 'prefix', 0, 0, axis_index_groups=cores)  16 us
    all_to_all x1, starting transfers between devices, local(): got = lax.all_to_all(parts.reshape(slots.shape), 'prefix', 0, 0)  11.5 us
    ppermute x1, waiting for transfers between devices, local(): start = lax.ppermute(start, ('prefix', 'resp'), back)  8.08 us
    pallas_call x7, Pallas kernels, call(): pl.pallas_call(kernel, out_shape=tuple(outs), in_specs=in_specs or [vmem]...  7.26 us
    ppermute x1, starting transfers between devices, local(): carried = lax.ppermute(carried, ('prefix', 'resp'), there)  7.02 us
    all_to_all x1, starting transfers between devices, local(): states = lax.all_to_all(states, 'prefix', 0, 0)  6.34 us
    ppermute x1, starting transfers between devices, local(): start = lax.ppermute(start, ('prefix', 'resp'), back)  6.04 us
    ppermute x1, waiting for transfers between devices, local(): carried = lax.ppermute(carried, ('prefix', 'resp'), there)  2.13 us
  transfers between devices with their start and end apart: 4, of which 3 were waited for; matrix products, arithmetic and copies ran while one was open for 0% of the time, Pallas kernels for 5%

profile of v4, /device:TPU:91, one launch (start us, length us, event | category | flops | bytes accessed | tf_op | source)
XLA Modules:
  0.0 67.1 jit_solution(10210830748028463346)
XLA Ops:
  0.6 2.1 %parts_kernel.1 = (bf16[2,8,2,32,128]{4,3,2,1,0:T(8,128)(2,1)}, f32[56,128]{1,0:T(8,128)}) custom-call(s32[64]{0:T(128)} %exps_in.1, bf16[128,512]{1,0:T(8,128)(2,1)} %pq.1, bf16[128,512]{1,0:T(8,128)(2,1)} %pk.3, bf16[128,512]{1,0:T(8,128)(2,1)} %pv.3, bf16[128,512]{1,0:T(8,128)(2,1)} %pg.3), custom_call_target="tpu_custom_call" | custom-call | flops 33554432 | bytes 815360 | tf_op jit(solution)/shard_map/parts_kernel/pallas_call | solution.py:255
  2.8 0.0 copy-start.3
  2.8 0.0 copy-start.4
  2.8 0.0 copy-start.2
  2.8 0.0 copy-start.5
  2.8 11.5 %all-to-all-start = ((bf16[32,32,128]{2,1,0:T(8,128)(2,1)}), bf16[32,32,128]{2,1,0:T(8,128)(2,1)S(1)}, u32[]{:S(2)}, u32[]{:S(2)}) async-start(bf16[32,32,128]{2,1,0:T(8,128)(2,1)} %bitcast.1), calls=%async_computation | async-start | bytes 524288 | tf_op jit(solution)/shard_map/all_to_all | solution.py:304
  15.0 0.0 copy-done.8
  15.0 0.0 copy-done.3
  15.0 0.0 copy-start
  15.0 0.0 copy-start.1
  15.0 0.2 carried_kernel.1
  15.3 7.0 %collective-permute-start = (bf16[16,16,128]{2,1,0:T(8,128)(2,1)S(1)}, bf16[16,16,128]{2,1,0:T(8,128)(2,1)S(1)}, u32[]{:S(2)}, u32[]{:S(2)}) collective-permute-start(bf16[16,16,128]{2,1,0:T(8,128)(2,1)S(1)} %get-tuple-element.26), channel_id=1, source_target_pairs={{0,160},{1,384},{2,320},{3,224},{4,128},{5,416},{6,288},{7,192},{8... | collective-permute-start | bytes 196616 | tf_op jit(solution)/shard_map/ppermute | solution.py:305
  22.4 1.0 %local_kernel.1 = (f32[128,512]{1,0:T(8,128)S(1)}, f32[128,512]{1,0:T(8,128)S(1)}, f32[128,512]{1,0:T(8,128)S(1)}, f32[8,128]{1,0:T(8,128)S(1)}) custom-call(f32[56,128]{1,0:T(8,128)S(1)} %copy-done.3, bf16[128,512]{1,0:T(8,128)(2,1)S(1)} %copy-done.5, bf16[128,512]{1,0:T(8,128)(2,1)S(1)} %copy-done, bf16[128,512]{1,0:T(8,128)(2,1)S(1)} %copy-done.1, ...), custom_call_target="tpu_custom_call" | custom-call | flops 83886080 | bytes 1343488 | tf_op jit(solution)/shard_map/local_kernel/pallas_call | solution.py:255
  23.4 2.1 %collective-permute-done.carried = bf16[16,16,128]{2,1,0:T(8,128)(2,1)S(1)} collective-permute-done((bf16[16,16,128]{2,1,0:T(8,128)(2,1)S(1)}, bf16[16,16,128]{2,1,0:T(8,128)(2,1)S(1)}, u32[]{:S(2)}, u32[]{:S(2)}) %collective-permute-start) | collective-permute-done | bytes 65568 | tf_op jit(solution)/shard_map/ppermute | solution.py:305
  25.5 1.2 %all-to-all-done.got = bf16[32,32,128]{2,1,0:T(8,128)(2,1)S(1)} async-done(((bf16[32,32,128]{2,1,0:T(8,128)(2,1)}), bf16[32,32,128]{2,1,0:T(8,128)(2,1)S(1)}, u32[]{:S(2)}, u32[]{:S(2)}) %all-to-all-start) | async-done | bytes 262176 | tf_op jit(solution)/shard_map/all_to_all | solution.py:304
  26.7 0.1 start_kernel.1
  26.8 16.0 %all_to_all.15.got_two = bf16[16,32,128]{2,1,0:T(8,128)(2,1)S(1)} all-to-all(bf16[16,32,128]{2,1,0:T(8,128)(2,1)S(1)} %start_kernel.1), channel_id=1, replica_groups={{0,32,64,96,128,160,192,224,256,288,320,352,384,416,448,480},{16,48,80,..., dimensions={0} | all-to-all | bytes 262144 | tf_op jit(solution)/shard_map/all_to_all | solution.py:312
  42.8 0.8 %states_kernel.1 = (bf16[32,32,128]{2,1,0:T(8,128)(2,1)}, bf16[16,16,128]{2,1,0:T(8,128)(2,1)S(1)}, f32[8,128]{1,0:T(8,128)S(1)}) custom-call(f32[56,128]{1,0:T(8,128)S(1)} %copy-done.3, bf16[32,32,128]{2,1,0:T(8,128)(2,1)S(1)} %all-to-all-done.got, bf16[16,32,128]{2,1,0:T(8,128)(2,1)S(1)} %all_to_all.15.got_two), custom_call_target="tpu_custom_call" | custom-call | flops 4194304 | bytes 753664 | tf_op jit(solution)/shard_map/states_kernel/pallas_call | solution.py:255
  43.6 6.3 %all-to-all-start.2 = ((bf16[32,32,128]{2,1,0:T(8,128)(2,1)}), bf16[32,32,128]{2,1,0:T(8,128)(2,1)S(1)}, u32[]{:S(2)}, u32[]{:S(2)}) async-start(bf16[32,32,128]{2,1,0:T(8,128)(2,1)} %get-tuple-element.28), calls=%async_computation.2 | async-start | bytes 524288 | tf_op jit(solution)/shard_map/all_to_all | solution.py:322
  49.9 6.0 %collective-permute-start.1 = (bf16[16,16,128]{2,1,0:T(8,128)(2,1)S(1)}, bf16[16,16,128]{2,1,0:T(8,128)(2,1)S(1)}, u32[]{:S(2)}, u32[]{:S(2)}) collective-permute-start(bf16[16,16,128]{2,1,0:T(8,128)(2,1)S(1)} %get-tuple-element.33), channel_id=1, source_target_pairs={{128,0},{384,1},{480,2},{160,3},{416,4},{448,5},{320,6},{64,7},{19... | collective-permute-start | bytes 196616 | tf_op jit(solution)/shard_map/ppermute | solution.py:323
  56.0 1.9 %resp_kernel.1 = (f32[256,256]{1,0:T(8,128)S(1)}, bf16[1,256,256]{2,1,0:T(8,128)(2,1)}, bf16[1,256,256]{2,1,0:T(8,128)(2,1)}) custom-call(f32[56,128]{1,0:T(8,128)S(1)} %copy-done.3, bf16[1,256,256]{2,1,0:T(8,128)(2,1)S(1)} %copy-done.4, bf16[1,256,256]{2,1,0:T(8,128)(2,1)S(1)} %copy-done.6, bf16[1,256,256]{2,1,0:T(8,128)(2,1)S(1)} %copy-done.7, ...), custom_call_target="tpu_custom_call" | custom-call | flops 117440512 | bytes 1081344 | tf_op jit(solution)/shard_map/resp_kernel/pallas_call | solution.py:255
  57.9 8.1 %collective-permute-done.1.start = bf16[16,16,128]{2,1,0:T(8,128)(2,1)S(1)} collective-permute-done((bf16[16,16,128]{2,1,0:T(8,128)(2,1)S(1)}, bf16[16,16,128]{2,1,0:T(8,128)(2,1)S(1)}, u32[]{:S(2)}, u32[]{:S(2)}) %collective-permute-start.1) | collective-permute-done | bytes 65568 | tf_op jit(solution)/shard_map/ppermute | solution.py:323
  65.9 0.0 all-to-all-done.2.states
  65.9 1.1 %final_kernel.1 = (bf16[128,512]{1,0:T(8,128)(2,1)}, bf16[128,512]{1,0:T(8,128)(2,1)}, bf16[128,512]{1,0:T(8,128)(2,1)}, bf16[1,256,256]{2,1,0:T(8,128)(2,1)}) custom-call(f32[56,128]{1,0:T(8,128)S(1)} %copy-done.3, bf16[128,512]{1,0:T(8,128)(2,1)S(1)} %copy-done, bf16[128,512]{1,0:T(8,128)(2,1)S(1)} %copy-done.1, bf16[128,512]{1,0:T(8,128)(2,1)S(1)} %copy-done.2, ...), custom_call_target="tpu_custom_call" | custom-call | flops 67108864 | bytes 2453504 | tf_op jit(solution)/shard_map/final_kernel/pallas_call | solution.py:255
  (10 shorter events, 0.0 us)
Async XLA Ops:
  0.6 14.4 %copy-start.8 = (bf16[1,256,256]{2,1,0:T(8,128)(2,1)S(1)}, bf16[1,256,256]{2,1,0:T(8,128)(2,1)}, u32[]{:S(2)}) copy-start(bf16[1,256,256]{2,1,0:T(8,128)(2,1)} %rg.1) | copy-start | bytes 393220
  2.8 12.2 %copy-start.3 = (f32[56,128]{1,0:T(8,128)S(1)}, f32[56,128]{1,0:T(8,128)}, u32[]{:S(2)}) copy-start(f32[56,128]{1,0:T(8,128)} %get-tuple-element.24.rates) | copy-start | bytes 86020
  2.8 12.2 %copy-start.4 = (bf16[1,256,256]{2,1,0:T(8,128)(2,1)S(1)}, bf16[1,256,256]{2,1,0:T(8,128)(2,1)}, u32[]{:S(2)}) copy-start(bf16[1,256,256]{2,1,0:T(8,128)(2,1)} %rq.3) | copy-start | bytes 393220
  2.8 19.5 %copy-start.2 = (bf16[128,512]{1,0:T(8,128)(2,1)S(1)}, bf16[128,512]{1,0:T(8,128)(2,1)}, u32[]{:S(2)}) copy-start(bf16[128,512]{1,0:T(8,128)(2,1)} %pg.3) | copy-start | bytes 393220
  2.8 19.5 %copy-start.5 = (bf16[128,512]{1,0:T(8,128)(2,1)S(1)}, bf16[128,512]{1,0:T(8,128)(2,1)}, u32[]{:S(2)}) copy-start(bf16[128,512]{1,0:T(8,128)(2,1)} %pq.1) | copy-start | bytes 393220
  2.8 23.9 %all-to-all-start = ((bf16[32,32,128]{2,1,0:T(8,128)(2,1)}), bf16[32,32,128]{2,1,0:T(8,128)(2,1)S(1)}, u32[]{:S(2)}, u32[]{:S(2)}) async-start(bf16[32,32,128]{2,1,0:T(8,128)(2,1)} %bitcast.1), calls=%async_computation | async-start | bytes 524288 | tf_op jit(solution)/shard_map/all_to_all | solution.py:304
  15.0 7.3 %copy-start = (bf16[128,512]{1,0:T(8,128)(2,1)S(1)}, bf16[128,512]{1,0:T(8,128)(2,1)}, u32[]{:S(2)}) copy-start(bf16[128,512]{1,0:T(8,128)(2,1)} %pk.3) | copy-start | bytes 393220
  15.0 7.3 %copy-start.1 = (bf16[128,512]{1,0:T(8,128)(2,1)S(1)}, bf16[128,512]{1,0:T(8,128)(2,1)}, u32[]{:S(2)}) copy-start(bf16[128,512]{1,0:T(8,128)(2,1)} %pv.3) | copy-start | bytes 393220
  15.3 10.2 %collective-permute-start = (bf16[16,16,128]{2,1,0:T(8,128)(2,1)S(1)}, bf16[16,16,128]{2,1,0:T(8,128)(2,1)S(1)}, u32[]{:S(2)}, u32[]{:S(2)}) collective-permute-start(bf16[16,16,128]{2,1,0:T(8,128)(2,1)S(1)} %get-tuple-element.26), channel_id=1, source_target_pairs={{0,160},{1,384},{2,320},{3,224},{4,128},{5,416},{6,288},{7,192},{8... | collective-permute-start | bytes 196616 | tf_op jit(solution)/shard_map/ppermute | solution.py:305
  43.6 12.4 %copy-start.6 = (bf16[1,256,256]{2,1,0:T(8,128)(2,1)S(1)}, bf16[1,256,256]{2,1,0:T(8,128)(2,1)}, u32[]{:S(2)}) copy-start(bf16[1,256,256]{2,1,0:T(8,128)(2,1)} %rk.1) | copy-start | bytes 393220
  43.6 12.4 %copy-start.7 = (bf16[1,256,256]{2,1,0:T(8,128)(2,1)S(1)}, bf16[1,256,256]{2,1,0:T(8,128)(2,1)}, u32[]{:S(2)}) copy-start(bf16[1,256,256]{2,1,0:T(8,128)(2,1)} %rv.1) | copy-start | bytes 393220
  43.6 22.4 %all-to-all-start.2 = ((bf16[32,32,128]{2,1,0:T(8,128)(2,1)}), bf16[32,32,128]{2,1,0:T(8,128)(2,1)S(1)}, u32[]{:S(2)}, u32[]{:S(2)}) async-start(bf16[32,32,128]{2,1,0:T(8,128)(2,1)} %get-tuple-element.28), calls=%async_computation.2 | async-start | bytes 524288 | tf_op jit(solution)/shard_map/all_to_all | solution.py:322
  49.9 16.0 %collective-permute-start.1 = (bf16[16,16,128]{2,1,0:T(8,128)(2,1)S(1)}, bf16[16,16,128]{2,1,0:T(8,128)(2,1)S(1)}, u32[]{:S(2)}, u32[]{:S(2)}) collective-permute-start(bf16[16,16,128]{2,1,0:T(8,128)(2,1)S(1)} %get-tuple-element.33), channel_id=1, source_target_pairs={{128,0},{384,1},{480,2},{160,3},{416,4},{448,5},{320,6},{64,7},{19... | collective-permute-start | bytes 196616 | tf_op jit(solution)/shard_map/ppermute | solution.py:323

commit v5 on v4

--- a/solution.py
+++ b/solution.py
@@ -36,33 +36,34 @@
     "f64ce758d02a913b",
 )
 SPREAD = (
-    "4cf5dea26b803791",
-    "4def75cb1089263a",
-    "c06e895da243b17f",
-    "fd67ec159b248a30",
-    "29d608b1fa437ec5",
-    "3b8e09af217c546d",
-    "d528c09af43be617",
-    "cd54b923ae618f70",
-    "9802ef73cd64ba15",
-    "6891fca25d374eb0",
-    "2a4b38d9076f15ec",
-    "b3a8c10de47f9256",
-    "fd57bc43ae618920",
-    "3ae4c8d509f612b7",
-    "709e64fd51a8c32b",
-    "d64ce7098f1ba532",
+    "nvf7hpa2go806e91",
+    "goefhpq82b193i0a",
+    "80hrb1jpa2iq934c",
+    "qd5h43j69b2ica1r",
+    "2td5jrb3lae6ksc4",
+    "7mfckuabltse645d",
+    "f4nuc0tvd7l8e6m5",
+    "9dnva81gue0m7f65",
+    "oa01ge86hp75df29",
+    "hp917oa2igf3bq80",
+    "2a9b1jc80hip34rq",
+    "b3jra29ed4isc15q",
+    "9bcdse45la6krt32",
+    "luc64td5fse7mkb3",
+    "5fmc6e8d70tu4lnv",
+    "e6duf7nv851a90mo",
 )
 
 
-def exchange_pairs(table):
+def exchange_pairs(table, turn):
     pairs = []
     for column in range(RESPS):
         for resp in range(RESPS):
-            chip = int(table[column][resp], 16)
-            for core in range(2):
-                response = (2 * column + core) * RESPS + resp
-                pairs.append((response, (2 * chip + core) * RESPS + column))
+            at, chip = divmod(int(table[column][resp], 32), 16)
+            if at == turn:
+                for core in range(2):
+                    response = (2 * column + core) * RESPS + resp
+                    pairs.append((response, (2 * chip + core) * RESPS + column))
     return sorted(pairs)
 
 
@@ -225,12 +226,13 @@
 
 
 def final_kernel(
-    rates, pk, pv, pg, states, pdq, pdk, pdv, masked, start, rdq, dq, dk, dv, resp_dq
+    rates, pk, pv, pg, states, pdq, pdk, pdv, masked, start, start_two, rdq, dq, dk, dv, resp_dq
 ):
     for h in range(PAIR):
         c = cut(h)
         rate = rate_row(rates, GROUP + h)
-        state = start[8 * h : 8 * h + 8].reshape(D, D)
+        cuts = slice(8 * h, 8 * h + 8)
+        state = (start[cuts] + start_two[cuts]).reshape(D, D)
         for j in range(2):
             weight = jnp.exp(-rate * (rows() + float(j * D + 1)))
             term = nt(masked[cut(j), c], state) * weight
@@ -320,10 +322,10 @@
         28 * cube,
     )
     states = lax.all_to_all(states, "prefix", 0, 0)
-    start = lax.ppermute(start, ("prefix", "resp"), back)
+    starts = [lax.ppermute(start, ("prefix", "resp"), pairs) for pairs in back]
     pre_dq, pre_dk, pre_dv, resp_dq = call(
         final_kernel,
-        [rates, pk, pv, pg, states, pdq, pdk, pdv, masked, start, rdq],
+        [rates, pk, pv, pg, states, pdq, pdk, pdv, masked, *starts, rdq],
         [shaped(flat, BF16)] * 3 + [resp_out],
         16 * cube,
     )
@@ -331,8 +333,8 @@
 
 
 def solution(mesh):
-    there = exchange_pairs(GATHER)
-    back = [(partner, response) for response, partner in exchange_pairs(SPREAD)]
+    there = exchange_pairs(GATHER, 0)
+    back = [[(b, a) for a, b in exchange_pairs(SPREAD, turn)] for turn in range(2)]
     prompt, response = P("prefix", "resp"), P("resp", None, "prefix")
     return jax.shard_map(
         functools.partial(local, there, back),

time: 67.5 us -> 66.9 us (level)
  the two profiles are of different devices: /device:TPU:91 before, /device:TPU:40 now
where the time goes in v5:
time: 66.9 us; the launch traced here: 66.5 us
  starting transfers between devices  24.8 us (37%)
  blocking collectives  19.3 us (29%)
  waiting for transfers between devices  13.6 us (20%)
  Pallas kernels  7.25 us (11%)
  between operations  1.47 us (2%)
    all_to_all x1, blocking collectives, local(): got_two = lax.all_to_all(sent, 'prefix', 0, 0, axis_index_groups=cores)  19.3 us
    all_to_all x1, starting transfers between devices, local(): got = lax.all_to_all(parts.reshape(slots.shape), 'prefix', 0, 0)  12.1 us
    ppermute x2, waiting for transfers between devices, local(): starts = [lax.ppermute(start, ('prefix', 'resp'), pairs) for pairs in back]  9.09 us
    pallas_call x7, Pallas kernels, call(): pl.pallas_call(kernel, out_shape=tuple(outs), in_specs=in_specs or [vmem]...  7.25 us
    ppermute x1, starting transfers between devices, local(): carried = lax.ppermute(carried, ('prefix', 'resp'), there)  5.37 us
    ppermute x1, waiting for transfers between devices, local(): carried = lax.ppermute(carried, ('prefix', 'resp'), there)  4.54 us
    all_to_all x1, starting transfers between devices, local(): states = lax.all_to_all(states, 'prefix', 0, 0)  4.39 us
    ppermute x2, starting transfers between devices, local(): starts = [lax.ppermute(start, ('prefix', 'resp'), pairs) for pairs in back]  2.94 us
  transfers between devices with their start and end apart: 5, of which 2 were waited for; matrix products, arithmetic and copies ran while one was open for 0% of the time, Pallas kernels for 5%

profile of v5, /device:TPU:40, one launch (start us, length us, event | category | flops | bytes accessed | tf_op | source)
XLA Modules:
  0.0 66.5 jit_solution(11521752641169082492)
XLA Ops:
  0.6 2.1 %parts_kernel.1 = (bf16[2,8,2,32,128]{4,3,2,1,0:T(8,128)(2,1)}, f32[56,128]{1,0:T(8,128)}) custom-call(s32[64]{0:T(128)} %exps_in.1, bf16[128,512]{1,0:T(8,128)(2,1)} %pq.1, bf16[128,512]{1,0:T(8,128)(2,1)} %pk.3, bf16[128,512]{1,0:T(8,128)(2,1)} %pv.3, bf16[128,512]{1,0:T(8,128)(2,1)} %pg.3), custom_call_target="tpu_custom_call" | custom-call | flops 33554432 | bytes 815360 | tf_op jit(solution)/shard_map/parts_kernel/pallas_call | solution.py:257
  2.8 0.0 copy-start.3
  2.8 0.0 copy-start.4
  2.8 0.0 copy-start.2
  2.8 0.0 copy-start.5
  2.8 12.1 %all-to-all-start = ((bf16[32,32,128]{2,1,0:T(8,128)(2,1)}), bf16[32,32,128]{2,1,0:T(8,128)(2,1)S(1)}, u32[]{:S(2)}, u32[]{:S(2)}) async-start(bf16[32,32,128]{2,1,0:T(8,128)(2,1)} %bitcast.1), calls=%async_computation | async-start | bytes 524288 | tf_op jit(solution)/shard_map/all_to_all | solution.py:306
  15.6 0.0 copy-start
  15.6 0.0 copy-start.1
  15.6 0.2 carried_kernel.1
  15.9 5.4 %collective-permute-start = (bf16[16,16,128]{2,1,0:T(8,128)(2,1)S(1)}, bf16[16,16,128]{2,1,0:T(8,128)(2,1)S(1)}, u32[]{:S(2)}, u32[]{:S(2)}) collective-permute-start(bf16[16,16,128]{2,1,0:T(8,128)(2,1)S(1)} %get-tuple-element.26), channel_id=1, source_target_pairs={{0,160},{1,384},{2,320},{3,224},{4,128},{5,416},{6,288},{7,192},{8... | collective-permute-start | bytes 196616 | tf_op jit(solution)/shard_map/ppermute | solution.py:307
  21.3 1.0 %local_kernel.1 = (f32[128,512]{1,0:T(8,128)S(1)}, f32[128,512]{1,0:T(8,128)S(1)}, f32[128,512]{1,0:T(8,128)S(1)}, f32[8,128]{1,0:T(8,128)S(1)}) custom-call(f32[56,128]{1,0:T(8,128)S(1)} %copy-done.3, bf16[128,512]{1,0:T(8,128)(2,1)S(1)} %copy-done.5, bf16[128,512]{1,0:T(8,128)(2,1)S(1)} %copy-done, bf16[128,512]{1,0:T(8,128)(2,1)S(1)} %copy-done.1, ...), custom_call_target="tpu_custom_call" | custom-call | flops 83886080 | bytes 1343488 | tf_op jit(solution)/shard_map/local_kernel/pallas_call | solution.py:257
  22.3 4.5 %collective-permute-done.carried = bf16[16,16,128]{2,1,0:T(8,128)(2,1)S(1)} collective-permute-done((bf16[16,16,128]{2,1,0:T(8,128)(2,1)S(1)}, bf16[16,16,128]{2,1,0:T(8,128)(2,1)S(1)}, u32[]{:S(2)}, u32[]{:S(2)}) %collective-permute-start) | collective-permute-done | bytes 65568 | tf_op jit(solution)/shard_map/ppermute | solution.py:307
  26.8 0.0 all-to-all-done.got
  26.8 0.1 start_kernel.1
  26.9 19.3 %all_to_all.15.got_two = bf16[16,32,128]{2,1,0:T(8,128)(2,1)S(1)} all-to-all(bf16[16,32,128]{2,1,0:T(8,128)(2,1)S(1)} %start_kernel.1), channel_id=1, replica_groups={{0,32,64,96,128,160,192,224,256,288,320,352,384,416,448,480},{16,48,80,..., dimensions={0} | all-to-all | bytes 262144 | tf_op jit(solution)/shard_map/all_to_all | solution.py:314
  46.2 0.8 %states_kernel.1 = (bf16[32,32,128]{2,1,0:T(8,128)(2,1)}, bf16[16,16,128]{2,1,0:T(8,128)(2,1)S(1)}, f32[8,128]{1,0:T(8,128)S(1)}) custom-call(f32[56,128]{1,0:T(8,128)S(1)} %copy-done.3, bf16[32,32,128]{2,1,0:T(8,128)(2,1)S(1)} %all-to-all-done.got, bf16[16,32,128]{2,1,0:T(8,128)(2,1)S(1)} %all_to_all.15.got_two), custom_call_target="tpu_custom_call" | custom-call | flops 4194304 | bytes 753664 | tf_op jit(solution)/shard_map/states_kernel/pallas_call | solution.py:257
  47.0 4.4 %all-to-all-start.2 = ((bf16[32,32,128]{2,1,0:T(8,128)(2,1)}), bf16[32,32,128]{2,1,0:T(8,128)(2,1)S(1)}, u32[]{:S(2)}, u32[]{:S(2)}) async-start(bf16[32,32,128]{2,1,0:T(8,128)(2,1)} %get-tuple-element.28), calls=%async_computation.2 | async-start | bytes 524288 | tf_op jit(solution)/shard_map/all_to_all | solution.py:324
  51.4 0.7 %collective-permute-start.2 = (bf16[16,16,128]{2,1,0:T(8,128)(2,1)S(1)}, bf16[16,16,128]{2,1,0:T(8,128)(2,1)S(1)}, u32[]{:S(2)}, u32[]{:S(2)}) collective-permute-start(bf16[16,16,128]{2,1,0:T(8,128)(2,1)S(1)} %get-tuple-element.33), channel_id=1, source_target_pairs={{224,0},{480,1},{32,4},{288,5},{0,8},{256,9},{240,16},{496,17},{48... | collective-permute-start | bytes 196616 | tf_op jit(solution)/shard_map/ppermute | solution.py:325
  52.0 2.3 %collective-permute-start.1 = (bf16[16,16,128]{2,1,0:T(8,128)(2,1)S(1)}, bf16[16,16,128]{2,1,0:T(8,128)(2,1)S(1)}, u32[]{:S(2)}, u32[]{:S(2)}) collective-permute-start(bf16[16,16,128]{2,1,0:T(8,128)(2,1)S(1)} %get-tuple-element.33), channel_id=1, source_target_pairs={{480,2},{224,3},{320,6},{64,7},{256,10},{0,11},{192,12},{448,13},{... | collective-permute-start | bytes 196616 | tf_op jit(solution)/shard_map/ppermute | solution.py:325
  54.3 1.9 %resp_kernel.1 = (f32[256,256]{1,0:T(8,128)S(1)}, bf16[1,256,256]{2,1,0:T(8,128)(2,1)}, bf16[1,256,256]{2,1,0:T(8,128)(2,1)}) custom-call(f32[56,128]{1,0:T(8,128)S(1)} %copy-done.3, bf16[1,256,256]{2,1,0:T(8,128)(2,1)S(1)} %copy-done.4, bf16[1,256,256]{2,1,0:T(8,128)(2,1)S(1)} %copy-done.6, bf16[1,256,256]{2,1,0:T(8,128)(2,1)S(1)} %copy-done.7, ...), custom_call_target="tpu_custom_call" | custom-call | flops 117440512 | bytes 1081344 | tf_op jit(solution)/shard_map/resp_kernel/pallas_call | solution.py:257
  56.2 0.0 collective-permute-done.2.start_two
  56.2 9.1 %collective-permute-done.1.start = bf16[16,16,128]{2,1,0:T(8,128)(2,1)S(1)} collective-permute-done((bf16[16,16,128]{2,1,0:T(8,128)(2,1)S(1)}, bf16[16,16,128]{2,1,0:T(8,128)(2,1)S(1)}, u32[]{:S(2)}, u32[]{:S(2)}) %collective-permute-start.1) | collective-permute-done | bytes 65568 | tf_op jit(solution)/shard_map/ppermute | solution.py:325
  65.3 0.0 all-to-all-done.2.states
  65.3 1.1 %final_kernel.1 = (bf16[128,512]{1,0:T(8,128)(2,1)}, bf16[128,512]{1,0:T(8,128)(2,1)}, bf16[128,512]{1,0:T(8,128)(2,1)}, bf16[1,256,256]{2,1,0:T(8,128)(2,1)}) custom-call(f32[56,128]{1,0:T(8,128)S(1)} %copy-done.3, bf16[128,512]{1,0:T(8,128)(2,1)S(1)} %copy-done, bf16[128,512]{1,0:T(8,128)(2,1)S(1)} %copy-done.1, bf16[128,512]{1,0:T(8,128)(2,1)S(1)} %copy-done.2, ...), custom_call_target="tpu_custom_call" | custom-call | flops 67108864 | bytes 2519040 | tf_op jit(solution)/shard_map/final_kernel/pallas_call | solution.py:257
  (12 shorter events, 0.0 us)
Async XLA Ops:
  0.6 14.9 %copy-start.8 = (bf16[1,256,256]{2,1,0:T(8,128)(2,1)S(1)}, bf16[1,256,256]{2,1,0:T(8,128)(2,1)}, u32[]{:S(2)}) copy-start(bf16[1,256,256]{2,1,0:T(8,128)(2,1)} %rg.1) | copy-start | bytes 393220
  2.8 12.8 %copy-start.3 = (f32[56,128]{1,0:T(8,128)S(1)}, f32[56,128]{1,0:T(8,128)}, u32[]{:S(2)}) copy-start(f32[56,128]{1,0:T(8,128)} %get-tuple-element.24.rates) | copy-start | bytes 86020
  2.8 12.8 %copy-start.4 = (bf16[1,256,256]{2,1,0:T(8,128)(2,1)S(1)}, bf16[1,256,256]{2,1,0:T(8,128)(2,1)}, u32[]{:S(2)}) copy-start(bf16[1,256,256]{2,1,0:T(8,128)(2,1)} %rq.3) | copy-start | bytes 393220
  2.8 18.4 %copy-start.2 = (bf16[128,512]{1,0:T(8,128)(2,1)S(1)}, bf16[128,512]{1,0:T(8,128)(2,1)}, u32[]{:S(2)}) copy-start(bf16[128,512]{1,0:T(8,128)(2,1)} %pg.3) | copy-start | bytes 393220
  2.8 18.4 %copy-start.5 = (bf16[128,512]{1,0:T(8,128)(2,1)S(1)}, bf16[128,512]{1,0:T(8,128)(2,1)}, u32[]{:S(2)}) copy-start(bf16[128,512]{1,0:T(8,128)(2,1)} %pq.1) | copy-start | bytes 393220
  2.8 24.0 %all-to-all-start = ((bf16[32,32,128]{2,1,0:T(8,128)(2,1)}), bf16[32,32,128]{2,1,0:T(8,128)(2,1)S(1)}, u32[]{:S(2)}, u32[]{:S(2)}) async-start(bf16[32,32,128]{2,1,0:T(8,128)(2,1)} %bitcast.1), calls=%async_computation | async-start | bytes 524288 | tf_op jit(solution)/shard_map/all_to_all | solution.py:306
  15.6 5.7 %copy-start = (bf16[128,512]{1,0:T(8,128)(2,1)S(1)}, bf16[128,512]{1,0:T(8,128)(2,1)}, u32[]{:S(2)}) copy-start(bf16[128,512]{1,0:T(8,128)(2,1)} %pk.3) | copy-start | bytes 393220
  15.6 5.7 %copy-start.1 = (bf16[128,512]{1,0:T(8,128)(2,1)S(1)}, bf16[128,512]{1,0:T(8,128)(2,1)}, u32[]{:S(2)}) copy-start(bf16[128,512]{1,0:T(8,128)(2,1)} %pv.3) | copy-start | bytes 393220
  15.9 11.0 %collective-permute-start = (bf16[16,16,128]{2,1,0:T(8,128)(2,1)S(1)}, bf16[16,16,128]{2,1,0:T(8,128)(2,1)S(1)}, u32[]{:S(2)}, u32[]{:S(2)}) collective-permute-start(bf16[16,16,128]{2,1,0:T(8,128)(2,1)S(1)} %get-tuple-element.26), channel_id=1, source_target_pairs={{0,160},{1,384},{2,320},{3,224},{4,128},{5,416},{6,288},{7,192},{8... | collective-permute-start | bytes 196616 | tf_op jit(solution)/shard_map/ppermute | solution.py:307
  47.0 7.4 %copy-start.6 = (bf16[1,256,256]{2,1,0:T(8,128)(2,1)S(1)}, bf16[1,256,256]{2,1,0:T(8,128)(2,1)}, u32[]{:S(2)}) copy-start(bf16[1,256,256]{2,1,0:T(8,128)(2,1)} %rk.1) | copy-start | bytes 393220
  47.0 7.4 %copy-start.7 = (bf16[1,256,256]{2,1,0:T(8,128)(2,1)S(1)}, bf16[1,256,256]{2,1,0:T(8,128)(2,1)}, u32[]{:S(2)}) copy-start(bf16[1,256,256]{2,1,0:T(8,128)(2,1)} %rv.1) | copy-start | bytes 393220
  47.0 18.3 %all-to-all-start.2 = ((bf16[32,32,128]{2,1,0:T(8,128)(2,1)}), bf16[32,32,128]{2,1,0:T(8,128)(2,1)S(1)}, u32[]{:S(2)}, u32[]{:S(2)}) async-start(bf16[32,32,128]{2,1,0:T(8,128)(2,1)} %get-tuple-element.28), calls=%async_computation.2 | async-start | bytes 524288 | tf_op jit(solution)/shard_map/all_to_all | solution.py:324
  51.4 4.8 %collective-permute-start.2 = (bf16[16,16,128]{2,1,0:T(8,128)(2,1)S(1)}, bf16[16,16,128]{2,1,0:T(8,128)(2,1)S(1)}, u32[]{:S(2)}, u32[]{:S(2)}) collective-permute-start(bf16[16,16,128]{2,1,0:T(8,128)(2,1)S(1)} %get-tuple-element.33), channel_id=1, source_target_pairs={{224,0},{480,1},{32,4},{288,5},{0,8},{256,9},{240,16},{496,17},{48... | collective-permute-start | bytes 196616 | tf_op jit(solution)/shard_map/ppermute | solution.py:325
  52.0 13.3 %collective-permute-start.1 = (bf16[16,16,128]{2,1,0:T(8,128)(2,1)S(1)}, bf16[16,16,128]{2,1,0:T(8,128)(2,1)S(1)}, u32[]{:S(2)}, u32[]{:S(2)}) collective-permute-start(bf16[16,16,128]{2,1,0:T(8,128)(2,1)S(1)} %get-tuple-element.33), channel_id=1, source_target_pairs={{480,2},{224,3},{320,6},{64,7},{256,10},{0,11},{192,12},{448,13},{... | collective-permute-start | bytes 196616 | tf_op jit(solution)/shard_map/ppermute | solution.py:325

commit v6 on v5

--- a/solution.py
+++ b/solution.py
@@ -167,20 +167,25 @@
     return nn(dscores, k), tn(dscores, q), tn(weights, g)
 
 
-def local_kernel(rates, pq, pk, pv, pg, pdq, pdk, pdv, token):
+def local_kernel(rates, pq, pk, pv, pg, pdq, pdk, pdv, w_in, w_out, token):
     token[...] = jnp.zeros_like(token)
     for h in range(GROUP):
         c = cut(h)
-        mask = decay_mask(rate_row(rates, h))
+        rate = rate_row(rates, h)
+        mask = decay_mask(rate)
+        w_in[:, c] = jnp.exp(-rate * (rows() + 1.0))
+        w_out[:, c] = jnp.exp(-rate * (float(D) - rows()))
         pdq[:, c], pdk[:, c], pdv[:, c] = local_grads(pq[:, c], pk[:, c], pv[:, c], pg[:, c], mask)
 
 
-def resp_kernel(rates, rq, rk, rv, masked, after, rdq, rdk, rdv):
+def resp_kernel(rates, rq, rk, rv, masked, after, rdq, rdk, rdv, w_resp):
     for h in range(PAIR):
         c = cut(h)
         rate = rate_row(rates, GROUP + h)
         mask = decay_mask(rate)
         g0, g1 = masked[cut(0), c], masked[cut(1), c]
+        for j in range(2):
+            w_resp[cut(j), c] = jnp.exp(-rate * (rows() + float(j * D + 1)))
         q0, q1 = rq[0, cut(0), c], rq[0, cut(1), c]
         k0, k1 = rk[0, cut(0), c], rk[0, cut(1), c]
         v0, v1 = rv[0, cut(0), c], rv[0, cut(1), c]
@@ -226,26 +231,24 @@
 
 
 def final_kernel(
-    rates, pk, pv, pg, states, pdq, pdk, pdv, masked, start, start_two, rdq, dq, dk, dv, resp_dq
+    w_in, w_out, w_resp, pk, pv, pg, states, pdq, pdk, pdv, masked, start, start_two, rdq, dq, dk, dv, resp_dq
 ):
     for h in range(PAIR):
         c = cut(h)
-        rate = rate_row(rates, GROUP + h)
         cuts = slice(8 * h, 8 * h + 8)
         state = (start[cuts] + start_two[cuts]).reshape(D, D)
         for j in range(2):
-            weight = jnp.exp(-rate * (rows() + float(j * D + 1)))
+            weight = w_resp[cut(j), c]
             term = nt(masked[cut(j), c], state) * weight
             resp_dq[0, cut(j), c] = (rdq[cut(j), c] + term).astype(BF16)
     for h in range(GROUP):
         c = cut(h)
-        rate = rate_row(rates, h)
         both = [states[owner(h, k)] for k in range(8)]
         state_in = jnp.concatenate([b[0:PART] for b in both], axis=0)
         state_out = jnp.concatenate([b[PART : 2 * PART] for b in both], axis=0)
-        weight = jnp.exp(-rate * (rows() + 1.0))
+        weight = w_in[:, c]
         dq[:, c] = (pdq[:, c] + nt(pg[:, c], state_in) * weight).astype(BF16)
-        weight = jnp.exp(-rate * (float(D) - rows()))
+        weight = w_out[:, c]
         dk[:, c] = (pdk[:, c] + nt(pv[:, c], state_out) * weight).astype(BF16)
         dv[:, c] = (pdv[:, c] + nn(pk[:, c], state_out) * weight).astype(BF16)
 
@@ -305,8 +308,8 @@
     )
     got = lax.all_to_all(parts.reshape(slots.shape), "prefix", 0, 0)
     carried = lax.ppermute(carried, ("prefix", "resp"), there)
-    pdq, pdk, pdv, before = call(
-        local_kernel, [rates, pq, pk, pv, pg], [shaped(flat, F32)] * 3 + [token], 20 * cube
+    pdq, pdk, pdv, w_in, w_out, before = call(
+        local_kernel, [rates, pq, pk, pv, pg], [shaped(flat, F32)] * 5 + [token], 20 * cube
     )
     sent = call(
         start_kernel, [rates, got, carried, before], [shaped((RESPS, 2 * PART, D), BF16)], cube
@@ -315,17 +318,17 @@
     states, start, after = call(
         states_kernel, [rates, got, got_two], [slots, pair, token], cube
     )
-    rdq, rdk, rdv = call(
+    rdq, rdk, rdv, w_resp = call(
         resp_kernel,
         [rates, rq, rk, rv, masked, after],
-        [shaped(rq.shape[1:], F32), resp_out, resp_out],
+        [shaped(rq.shape[1:], F32), resp_out, resp_out, shaped(rq.shape[1:], F32)],
         28 * cube,
     )
     states = lax.all_to_all(states, "prefix", 0, 0)
     starts = [lax.ppermute(start, ("prefix", "resp"), pairs) for pairs in back]
     pre_dq, pre_dk, pre_dv, resp_dq = call(
         final_kernel,
-        [rates, pk, pv, pg, states, pdq, pdk, pdv, masked, *starts, rdq],
+        [w_in, w_out, w_resp, pk, pv, pg, states, pdq, pdk, pdv, masked, *starts, rdq],
         [shaped(flat, BF16)] * 3 + [resp_out],
         16 * cube,
     )

time: 66.9 us -> 66.9 us (level)
  no operation moved by 1% of the time
where the time goes in v6:
time: 66.9 us; the launch traced here: 66.5 us
  starting transfers between devices  24.8 us (37%)
  blocking collectives  19.3 us (29%)
  waiting for transfers between devices  13.6 us (20%)
  Pallas kernels  7.27 us (11%)
  between operations  1.47 us (2%)
    all_to_all x1, blocking collectives, local(): got_two = lax.all_to_all(sent, 'prefix', 0, 0, axis_index_groups=cores)  19.3 us
    all_to_all x1, starting transfers between devices, local(): got = lax.all_to_all(parts.reshape(slots.shape), 'prefix', 0, 0)  12.1 us
    ppermute x2, waiting for transfers between devices, local(): starts = [lax.ppermute(start, ('prefix', 'resp'), pairs) for pairs in back]  9.08 us
    pallas_call x7, Pallas kernels, call(): pl.pallas_call(kernel, out_shape=tuple(outs), in_specs=in_specs or [vmem]...  7.27 us
    ppermute x1, starting transfers between devices, local(): carried = lax.ppermute(carried, ('prefix', 'resp'), there)  5.37 us
    ppermute x1, waiting for transfers between devices, local(): carried = lax.ppermute(carried, ('prefix', 'resp'), there)  4.53 us
    all_to_all x1, starting transfers between devices, local(): states = lax.all_to_all(states, 'prefix', 0, 0)  4.39 us
    ppermute x2, starting transfers between devices, local(): starts = [lax.ppermute(start, ('prefix', 'resp'), pairs) for pairs in back]  2.94 us
  transfers between devices with their start and end apart: 5, of which 2 were waited for; matrix products, arithmetic and copies ran while one was open for 0% of the time, Pallas kernels for 5%

profile of v6, /device:TPU:40, one launch (start us, length us, event | category | flops | bytes accessed | tf_op | source)
XLA Modules:
  0.0 66.5 jit_solution(11208332532638873457)
XLA Ops:
  0.6 2.1 %parts_kernel.1 = (bf16[2,8,2,32,128]{4,3,2,1,0:T(8,128)(2,1)}, f32[56,128]{1,0:T(8,128)}) custom-call(s32[64]{0:T(128)} %exps_in.1, bf16[128,512]{1,0:T(8,128)(2,1)} %pq.1, bf16[128,512]{1,0:T(8,128)(2,1)} %pk.3, bf16[128,512]{1,0:T(8,128)(2,1)} %pv.3, bf16[128,512]{1,0:T(8,128)(2,1)} %pg.3), custom_call_target="tpu_custom_call" | custom-call | flops 33554432 | bytes 815360 | tf_op jit(solution)/shard_map/parts_kernel/pallas_call | solution.py:260
  2.8 0.0 copy-start.3
  2.8 0.0 copy-start.4
  2.8 0.0 copy-start.2
  2.8 0.0 copy-start.5
  2.8 12.1 %all-to-all-start = ((bf16[32,32,128]{2,1,0:T(8,128)(2,1)}), bf16[32,32,128]{2,1,0:T(8,128)(2,1)S(1)}, u32[]{:S(2)}, u32[]{:S(2)}) async-start(bf16[32,32,128]{2,1,0:T(8,128)(2,1)} %bitcast.1), calls=%async_computation | async-start | bytes 524288 | tf_op jit(solution)/shard_map/all_to_all | solution.py:309
  15.6 0.0 copy-start
  15.6 0.0 copy-start.1
  15.6 0.2 carried_kernel.1
  15.9 5.4 %collective-permute-start = (bf16[16,16,128]{2,1,0:T(8,128)(2,1)S(1)}, bf16[16,16,128]{2,1,0:T(8,128)(2,1)S(1)}, u32[]{:S(2)}, u32[]{:S(2)}) collective-permute-start(bf16[16,16,128]{2,1,0:T(8,128)(2,1)S(1)} %get-tuple-element.32), channel_id=1, source_target_pairs={{0,160},{1,384},{2,320},{3,224},{4,128},{5,416},{6,288},{7,192},{8... | collective-permute-start | bytes 196616 | tf_op jit(solution)/shard_map/ppermute | solution.py:310
  21.3 1.0 %local_kernel.1 = (f32[128,512]{1,0:T(8,128)S(1)}, f32[128,512]{1,0:T(8,128)S(1)}, f32[128,512]{1,0:T(8,128)S(1)}, f32[128,512]{1,0:T(8,128)S(1)}, f32[128,512]{1,0:T(8,128)S(1)}, /*index=5*/f32[8,128]{1,0:T(8,128)S(1)}) custom-call(f32[56,128]{1,0:T(8,128)S(1)} %copy-done.3, bf16[128,512]{1,0:T(8,128)(2,1)S(1)} %copy-done.5, bf16[128,512]{1,0:T(8,128)(2,1)S(1)} %copy-done, ...), custom_call_target="tpu_custom_call" | custom-call | flops 83886080 | bytes 1867776 | tf_op jit(solution)/shard_map/local_kernel/pallas_call | solution.py:260
  22.3 4.5 %collective-permute-done.carried = bf16[16,16,128]{2,1,0:T(8,128)(2,1)S(1)} collective-permute-done((bf16[16,16,128]{2,1,0:T(8,128)(2,1)S(1)}, bf16[16,16,128]{2,1,0:T(8,128)(2,1)S(1)}, u32[]{:S(2)}, u32[]{:S(2)}) %collective-permute-start) | collective-permute-done | bytes 65568 | tf_op jit(solution)/shard_map/ppermute | solution.py:310
  26.8 0.0 all-to-all-done.got
  26.8 0.1 start_kernel.1
  26.9 19.3 %all_to_all.15.got_two = bf16[16,32,128]{2,1,0:T(8,128)(2,1)S(1)} all-to-all(bf16[16,32,128]{2,1,0:T(8,128)(2,1)S(1)} %start_kernel.1), channel_id=1, replica_groups={{0,32,64,96,128,160,192,224,256,288,320,352,384,416,448,480},{16,48,80,..., dimensions={0} | all-to-all | bytes 262144 | tf_op jit(solution)/shard_map/all_to_all | solution.py:317
  46.2 0.8 %states_kernel.1 = (bf16[32,32,128]{2,1,0:T(8,128)(2,1)}, bf16[16,16,128]{2,1,0:T(8,128)(2,1)S(1)}, f32[8,128]{1,0:T(8,128)S(1)}) custom-call(f32[56,128]{1,0:T(8,128)S(1)} %copy-done.3, bf16[32,32,128]{2,1,0:T(8,128)(2,1)S(1)} %all-to-all-done.got, bf16[16,32,128]{2,1,0:T(8,128)(2,1)S(1)} %all_to_all.15.got_two), custom_call_target="tpu_custom_call" | custom-call | flops 4194304 | bytes 753664 | tf_op jit(solution)/shard_map/states_kernel/pallas_call | solution.py:260
  47.0 4.4 %all-to-all-start.2 = ((bf16[32,32,128]{2,1,0:T(8,128)(2,1)}), bf16[32,32,128]{2,1,0:T(8,128)(2,1)S(1)}, u32[]{:S(2)}, u32[]{:S(2)}) async-start(bf16[32,32,128]{2,1,0:T(8,128)(2,1)} %get-tuple-element.36), calls=%async_computation.2 | async-start | bytes 524288 | tf_op jit(solution)/shard_map/all_to_all | solution.py:327
  51.4 0.7 %collective-permute-start.2 = (bf16[16,16,128]{2,1,0:T(8,128)(2,1)S(1)}, bf16[16,16,128]{2,1,0:T(8,128)(2,1)S(1)}, u32[]{:S(2)}, u32[]{:S(2)}) collective-permute-start(bf16[16,16,128]{2,1,0:T(8,128)(2,1)S(1)} %get-tuple-element.40), channel_id=1, source_target_pairs={{224,0},{480,1},{32,4},{288,5},{0,8},{256,9},{240,16},{496,17},{48... | collective-permute-start | bytes 196616 | tf_op jit(solution)/shard_map/ppermute | solution.py:328
  52.0 2.3 %collective-permute-start.1 = (bf16[16,16,128]{2,1,0:T(8,128)(2,1)S(1)}, bf16[16,16,128]{2,1,0:T(8,128)(2,1)S(1)}, u32[]{:S(2)}, u32[]{:S(2)}) collective-permute-start(bf16[16,16,128]{2,1,0:T(8,128)(2,1)S(1)} %get-tuple-element.40), channel_id=1, source_target_pairs={{480,2},{224,3},{320,6},{64,7},{256,10},{0,11},{192,12},{448,13},{... | collective-permute-start | bytes 196616 | tf_op jit(solution)/shard_map/ppermute | solution.py:328
  54.3 1.9 %resp_kernel.1 = (f32[256,256]{1,0:T(8,128)S(1)}, bf16[1,256,256]{2,1,0:T(8,128)(2,1)}, bf16[1,256,256]{2,1,0:T(8,128)(2,1)}, f32[256,256]{1,0:T(8,128)S(1)}) custom-call(f32[56,128]{1,0:T(8,128)S(1)} %copy-done.3, bf16[1,256,256]{2,1,0:T(8,128)(2,1)S(1)} %copy-done.4, bf16[1,256,256]{2,1,0:T(8,128)(2,1)S(1)} %copy-done.6, ...), custom_call_target="tpu_custom_call" | custom-call | flops 117440512 | bytes 1343488 | tf_op jit(solution)/shard_map/resp_kernel/pallas_call | solution.py:260
  56.2 0.0 collective-permute-done.2.start_two
  56.2 9.1 %collective-permute-done.1.start = bf16[16,16,128]{2,1,0:T(8,128)(2,1)S(1)} collective-permute-done((bf16[16,16,128]{2,1,0:T(8,128)(2,1)S(1)}, bf16[16,16,128]{2,1,0:T(8,128)(2,1)S(1)}, u32[]{:S(2)}, u32[]{:S(2)}) %collective-permute-start.1) | collective-permute-done | bytes 65568 | tf_op jit(solution)/shard_map/ppermute | solution.py:328
  65.3 0.0 all-to-all-done.2.states
  65.3 1.2 %final_kernel.1 = (bf16[128,512]{1,0:T(8,128)(2,1)}, bf16[128,512]{1,0:T(8,128)(2,1)}, bf16[128,512]{1,0:T(8,128)(2,1)}, bf16[1,256,256]{2,1,0:T(8,128)(2,1)}) custom-call(f32[128,512]{1,0:T(8,128)S(1)} %get-tuple-element.28.w_in, f32[128,512]{1,0:T(8,128)S(1)} %get-tuple-element.29.w_out, f32[256,256]{1,0:T(8,128)S(1)} %get-tuple-element.35.w_resp, ...), custom_call_target="tpu_custom_call" | custom-call | flops 67108864 | bytes 3276800 | tf_op jit(solution)/shard_map/final_kernel/pallas_call | solution.py:260
  (12 shorter events, 0.0 us)
Async XLA Ops:
  0.6 14.9 %copy-start.8 = (bf16[1,256,256]{2,1,0:T(8,128)(2,1)S(1)}, bf16[1,256,256]{2,1,0:T(8,128)(2,1)}, u32[]{:S(2)}) copy-start(bf16[1,256,256]{2,1,0:T(8,128)(2,1)} %rg.1) | copy-start | bytes 393220
  2.8 12.8 %copy-start.3 = (f32[56,128]{1,0:T(8,128)S(1)}, f32[56,128]{1,0:T(8,128)}, u32[]{:S(2)}) copy-start(f32[56,128]{1,0:T(8,128)} %get-tuple-element.27.rates) | copy-start | bytes 86020
  2.8 12.8 %copy-start.4 = (bf16[1,256,256]{2,1,0:T(8,128)(2,1)S(1)}, bf16[1,256,256]{2,1,0:T(8,128)(2,1)}, u32[]{:S(2)}) copy-start(bf16[1,256,256]{2,1,0:T(8,128)(2,1)} %rq.3) | copy-start | bytes 393220
  2.8 18.4 %copy-start.2 = (bf16[128,512]{1,0:T(8,128)(2,1)S(1)}, bf16[128,512]{1,0:T(8,128)(2,1)}, u32[]{:S(2)}) copy-start(bf16[128,512]{1,0:T(8,128)(2,1)} %pg.3) | copy-start | bytes 393220
  2.8 18.4 %copy-start.5 = (bf16[128,512]{1,0:T(8,128)(2,1)S(1)}, bf16[128,512]{1,0:T(8,128)(2,1)}, u32[]{:S(2)}) copy-start(bf16[128,512]{1,0:T(8,128)(2,1)} %pq.1) | copy-start | bytes 393220
  2.8 24.0 %all-to-all-start = ((bf16[32,32,128]{2,1,0:T(8,128)(2,1)}), bf16[32,32,128]{2,1,0:T(8,128)(2,1)S(1)}, u32[]{:S(2)}, u32[]{:S(2)}) async-start(bf16[32,32,128]{2,1,0:T(8,128)(2,1)} %bitcast.1), calls=%async_computation | async-start | bytes 524288 | tf_op jit(solution)/shard_map/all_to_all | solution.py:309
  15.6 5.7 %copy-start = (bf16[128,512]{1,0:T(8,128)(2,1)S(1)}, bf16[128,512]{1,0:T(8,128)(2,1)}, u32[]{:S(2)}) copy-start(bf16[128,512]{1,0:T(8,128)(2,1)} %pk.3) | copy-start | bytes 393220
  15.6 5.7 %copy-start.1 = (bf16[128,512]{1,0:T(8,128)(2,1)S(1)}, bf16[128,512]{1,0:T(8,128)(2,1)}, u32[]{:S(2)}) copy-start(bf16[128,512]{1,0:T(8,128)(2,1)} %pv.3) | copy-start | bytes 393220
  15.9 11.0 %collective-permute-start = (bf16[16,16,128]{2,1,0:T(8,128)(2,1)S(1)}, bf16[16,16,128]{2,1,0:T(8,128)(2,1)S(1)}, u32[]{:S(2)}, u32[]{:S(2)}) collective-permute-start(bf16[16,16,128]{2,1,0:T(8,128)(2,1)S(1)} %get-tuple-element.32), channel_id=1, source_target_pairs={{0,160},{1,384},{2,320},{3,224},{4,128},{5,416},{6,288},{7,192},{8... | collective-permute-start | bytes 196616 | tf_op jit(solution)/shard_map/ppermute | solution.py:310
  47.0 7.4 %copy-start.6 = (bf16[1,256,256]{2,1,0:T(8,128)(2,1)S(1)}, bf16[1,256,256]{2,1,0:T(8,128)(2,1)}, u32[]{:S(2)}) copy-start(bf16[1,256,256]{2,1,0:T(8,128)(2,1)} %rk.1) | copy-start | bytes 393220
  47.0 7.4 %copy-start.7 = (bf16[1,256,256]{2,1,0:T(8,128)(2,1)S(1)}, bf16[1,256,256]{2,1,0:T(8,128)(2,1)}, u32[]{:S(2)}) copy-start(bf16[1,256,256]{2,1,0:T(8,128)(2,1)} %rv.1) | copy-start | bytes 393220
  47.0 18.3 %all-to-all-start.2 = ((bf16[32,32,128]{2,1,0:T(8,128)(2,1)}), bf16[32,32,128]{2,1,0:T(8,128)(2,1)S(1)}, u32[]{:S(2)}, u32[]{:S(2)}) async-start(bf16[32,32,128]{2,1,0:T(8,128)(2,1)} %get-tuple-element.36), calls=%async_computation.2 | async-start | bytes 524288 | tf_op jit(solution)/shard_map/all_to_all | solution.py:327
  51.4 4.9 %collective-permute-start.2 = (bf16[16,16,128]{2,1,0:T(8,128)(2,1)S(1)}, bf16[16,16,128]{2,1,0:T(8,128)(2,1)S(1)}, u32[]{:S(2)}, u32[]{:S(2)}) collective-permute-start(bf16[16,16,128]{2,1,0:T(8,128)(2,1)S(1)} %get-tuple-element.40), channel_id=1, source_target_pairs={{224,0},{480,1},{32,4},{288,5},{0,8},{256,9},{240,16},{496,17},{48... | collective-permute-start | bytes 196616 | tf_op jit(solution)/shard_map/ppermute | solution.py:328
  52.0 13.3 %collective-permute-start.1 = (bf16[16,16,128]{2,1,0:T(8,128)(2,1)S(1)}, bf16[16,16,128]{2,1,0:T(8,128)(2,1)S(1)}, u32[]{:S(2)}, u32[]{:S(2)}) collective-permute-start(bf16[16,16,128]{2,1,0:T(8,128)(2,1)S(1)} %get-tuple-element.40), channel_id=1, source_target_pairs={{480,2},{224,3},{320,6},{64,7},{256,10},{0,11},{192,12},{448,13},{... | collective-permute-start | bytes 196616 | tf_op jit(solution)/shard_map/ppermute | solution.py:328

commit v7 on v5

--- a/solution.py
+++ b/solution.py
@@ -175,7 +175,8 @@
         pdq[:, c], pdk[:, c], pdv[:, c] = local_grads(pq[:, c], pk[:, c], pv[:, c], pg[:, c], mask)
 
 
-def resp_kernel(rates, rq, rk, rv, masked, after, rdq, rdk, rdv):
+def resp_kernel(rates, rq, rk, rv, masked, after, rdq, rdk, rdv, token):
+    token[...] = jnp.zeros_like(token)
     for h in range(PAIR):
         c = cut(h)
         rate = rate_row(rates, GROUP + h)
@@ -208,7 +209,7 @@
         out[j, PART : 2 * PART] = carried[j]
 
 
-def states_kernel(rates, got, got_two, out, start, token):
+def states_kernel(rates, got, got_two, out, start):
     decay = rates[48:49]
     ahead = jnp.zeros((PART, D), F32)
     behind = jnp.zeros((PART, D), F32)
@@ -222,7 +223,6 @@
         behind = behind * decay + got[e, PART : 2 * PART].astype(F32)
     for j in range(RESPS):
         start[j] = got_two[j, 0:PART]
-    token[...] = jnp.zeros_like(token)
 
 
 def final_kernel(
@@ -308,19 +308,17 @@
     pdq, pdk, pdv, before = call(
         local_kernel, [rates, pq, pk, pv, pg], [shaped(flat, F32)] * 3 + [token], 20 * cube
     )
+    rdq, rdk, rdv, after = call(
+        resp_kernel,
+        [rates, rq, rk, rv, masked, before],
+        [shaped(rq.shape[1:], F32), resp_out, resp_out, token],
+        28 * cube,
+    )
     sent = call(
-        start_kernel, [rates, got, carried, before], [shaped((RESPS, 2 * PART, D), BF16)], cube
+        start_kernel, [rates, got, carried, after], [shaped((RESPS, 2 * PART, D), BF16)], cube
     )
     got_two = lax.all_to_all(sent, "prefix", 0, 0, axis_index_groups=cores)
-    states, start, after = call(
-        states_kernel, [rates, got, got_two], [slots, pair, token], cube
-    )
-    rdq, rdk, rdv = call(
-        resp_kernel,
-        [rates, rq, rk, rv, masked, after],
-        [shaped(rq.shape[1:], F32), resp_out, resp_out],
-        28 * cube,
-    )
+    states, start = call(states_kernel, [rates, got, got_two], [slots, pair], cube)
     states = lax.all_to_all(states, "prefix", 0, 0)
     starts = [lax.ppermute(start, ("prefix", "resp"), pairs) for pairs in back]
     pre_dq, pre_dk, pre_dv, resp_dq = call(

time: 66.9 us -> 66.9 us (level)
    ppermute x2, waiting for transfers between devices: 9.09 us -> 11 us  [local(): starts = [lax.ppermute(start, ('prefix', 'resp'), pairs) for pairs in back]]
    ppermute x1, waiting for transfers between devices: 4.54 us -> 2.68 us  [local(): carried = lax.ppermute(carried, ('prefix', 'resp'), there)]
where the time goes in v7:
time: 66.9 us; the launch traced here: 66.5 us
  starting transfers between devices  24.8 us (37%)
  blocking collectives  19.2 us (29%)
  waiting for transfers between devices  13.7 us (20%)
  Pallas kernels  7.25 us (11%)
  between operations  1.49 us (2%)
    all_to_all x1, blocking collectives, local(): got_two = lax.all_to_all(sent, 'prefix', 0, 0, axis_index_groups=cores)  19.2 us
    all_to_all x1, starting transfers between devices, local(): got = lax.all_to_all(parts.reshape(slots.shape), 'prefix', 0, 0)  12.1 us
    ppermute x2, waiting for transfers between devices, local(): starts = [lax.ppermute(start, ('prefix', 'resp'), pairs) for pairs in back]  11 us
    pallas_call x7, Pallas kernels, call(): pl.pallas_call(kernel, out_shape=tuple(outs), in_specs=in_specs or [vmem]...  7.25 us
    ppermute x1, starting transfers between devices, local(): carried = lax.ppermute(carried, ('prefix', 'resp'), there)  5.5 us
    all_to_all x1, starting transfers between devices, local(): states = lax.all_to_all(states, 'prefix', 0, 0)  4.25 us
    ppermute x2, starting transfers between devices, local(): starts = [lax.ppermute(start, ('prefix', 'resp'), pairs) for pairs in back]  2.94 us
    ppermute x1, waiting for transfers between devices, local(): carried = lax.ppermute(carried, ('prefix', 'resp'), there)  2.68 us
  transfers between devices with their start and end apart: 5, of which 2 were waited for; matrix products, arithmetic and copies ran while one was open for 0% of the time, Pallas kernels for 5%

profile of v7, /device:TPU:40, one launch (start us, length us, event | category | flops | bytes accessed | tf_op | source)
XLA Modules:
  0.0 66.5 jit_solution(14251860784515441476)
XLA Ops:
  0.6 2.1 %parts_kernel.1 = (bf16[2,8,2,32,128]{4,3,2,1,0:T(8,128)(2,1)}, f32[56,128]{1,0:T(8,128)}) custom-call(s32[64]{0:T(128)} %exps_in.1, bf16[128,512]{1,0:T(8,128)(2,1)} %pq.1, bf16[128,512]{1,0:T(8,128)(2,1)} %pk.3, bf16[128,512]{1,0:T(8,128)(2,1)} %pv.3, bf16[128,512]{1,0:T(8,128)(2,1)} %pg.3), custom_call_target="tpu_custom_call" | custom-call | flops 33554432 | bytes 815360 | tf_op jit(solution)/shard_map/parts_kernel/pallas_call | solution.py:257
  2.8 0.0 copy-start.3
  2.8 0.0 copy-start.4
  2.8 0.0 copy-start.2
  2.8 0.0 copy-start.5
  2.8 12.1 %all-to-all-start = ((bf16[32,32,128]{2,1,0:T(8,128)(2,1)}), bf16[32,32,128]{2,1,0:T(8,128)(2,1)S(1)}, u32[]{:S(2)}, u32[]{:S(2)}) async-start(bf16[32,32,128]{2,1,0:T(8,128)(2,1)} %bitcast.1), calls=%async_computation | async-start | bytes 524288 | tf_op jit(solution)/shard_map/all_to_all | solution.py:306
  15.6 0.0 copy-start
  15.6 0.0 copy-start.1
  15.6 0.2 carried_kernel.1
  15.9 0.0 copy-start.6
  15.9 0.0 copy-start.7
  15.9 5.5 %collective-permute-start = (bf16[16,16,128]{2,1,0:T(8,128)(2,1)S(1)}, bf16[16,16,128]{2,1,0:T(8,128)(2,1)S(1)}, u32[]{:S(2)}, u32[]{:S(2)}) collective-permute-start(bf16[16,16,128]{2,1,0:T(8,128)(2,1)S(1)} %get-tuple-element.26), channel_id=1, source_target_pairs={{0,160},{1,384},{2,320},{3,224},{4,128},{5,416},{6,288},{7,192},{8... | collective-permute-start | bytes 196616 | tf_op jit(solution)/shard_map/ppermute | solution.py:307
  21.4 1.0 %local_kernel.1 = (f32[128,512]{1,0:T(8,128)S(1)}, f32[128,512]{1,0:T(8,128)S(1)}, f32[128,512]{1,0:T(8,128)S(1)}, f32[8,128]{1,0:T(8,128)S(1)}) custom-call(f32[56,128]{1,0:T(8,128)S(1)} %copy-done.3, bf16[128,512]{1,0:T(8,128)(2,1)S(1)} %copy-done.5, bf16[128,512]{1,0:T(8,128)(2,1)S(1)} %copy-done, bf16[128,512]{1,0:T(8,128)(2,1)S(1)} %copy-done.1, ...), custom_call_target="tpu_custom_call" | custom-call | flops 83886080 | bytes 1343488 | tf_op jit(solution)/shard_map/local_kernel/pallas_call | solution.py:257
  22.5 1.9 %resp_kernel.1 = (f32[256,256]{1,0:T(8,128)S(1)}, bf16[1,256,256]{2,1,0:T(8,128)(2,1)}, bf16[1,256,256]{2,1,0:T(8,128)(2,1)}, f32[8,128]{1,0:T(8,128)S(1)}) custom-call(f32[56,128]{1,0:T(8,128)S(1)} %copy-done.3, bf16[1,256,256]{2,1,0:T(8,128)(2,1)S(1)} %copy-done.4, bf16[1,256,256]{2,1,0:T(8,128)(2,1)S(1)} %copy-done.6, bf16[1,256,256]{2,1,0:T(8,128)(2,1)S(1)} %copy-done.7, ...), custom_call_target="tpu_custom_call" | custom-call | flops 117440512 | bytes 1085440 | tf_op jit(solution)/shard_map/resp_kernel/pallas_call | solution.py:257
  24.3 2.7 %collective-permute-done.carried = bf16[16,16,128]{2,1,0:T(8,128)(2,1)S(1)} collective-permute-done((bf16[16,16,128]{2,1,0:T(8,128)(2,1)S(1)}, bf16[16,16,128]{2,1,0:T(8,128)(2,1)S(1)}, u32[]{:S(2)}, u32[]{:S(2)}) %collective-permute-start) | collective-permute-done | bytes 65568 | tf_op jit(solution)/shard_map/ppermute | solution.py:307
  27.0 0.1 start_kernel.1
  27.1 19.2 %all_to_all.15.got_two = bf16[16,32,128]{2,1,0:T(8,128)(2,1)S(1)} all-to-all(bf16[16,32,128]{2,1,0:T(8,128)(2,1)S(1)} %start_kernel.1), channel_id=1, replica_groups={{0,32,64,96,128,160,192,224,256,288,320,352,384,416,448,480},{16,48,80,..., dimensions={0} | all-to-all | bytes 262144 | tf_op jit(solution)/shard_map/all_to_all | solution.py:320
  46.3 0.8 %states_kernel.1 = (bf16[32,32,128]{2,1,0:T(8,128)(2,1)}, bf16[16,16,128]{2,1,0:T(8,128)(2,1)S(1)}) custom-call(f32[56,128]{1,0:T(8,128)S(1)} %copy-done.3, bf16[32,32,128]{2,1,0:T(8,128)(2,1)S(1)} %all-to-all-done.got, bf16[16,32,128]{2,1,0:T(8,128)(2,1)S(1)} %all_to_all.15.got_two), custom_call_target="tpu_custom_call" | custom-call | flops 4194304 | bytes 749568 | tf_op jit(solution)/shard_map/states_kernel/pallas_call | solution.py:257
  47.1 4.3 %all-to-all-start.2 = ((bf16[32,32,128]{2,1,0:T(8,128)(2,1)}), bf16[32,32,128]{2,1,0:T(8,128)(2,1)S(1)}, u32[]{:S(2)}, u32[]{:S(2)}) async-start(bf16[32,32,128]{2,1,0:T(8,128)(2,1)} %get-tuple-element.30), calls=%async_computation.2 | async-start | bytes 524288 | tf_op jit(solution)/shard_map/all_to_all | solution.py:322
  51.4 0.7 %collective-permute-start.2 = (bf16[16,16,128]{2,1,0:T(8,128)(2,1)S(1)}, bf16[16,16,128]{2,1,0:T(8,128)(2,1)S(1)}, u32[]{:S(2)}, u32[]{:S(2)}) collective-permute-start(bf16[16,16,128]{2,1,0:T(8,128)(2,1)S(1)} %get-tuple-element.34), channel_id=1, source_target_pairs={{224,0},{480,1},{32,4},{288,5},{0,8},{256,9},{240,16},{496,17},{48... | collective-permute-start | bytes 196616 | tf_op jit(solution)/shard_map/ppermute | solution.py:323
  52.1 2.3 %collective-permute-start.1 = (bf16[16,16,128]{2,1,0:T(8,128)(2,1)S(1)}, bf16[16,16,128]{2,1,0:T(8,128)(2,1)S(1)}, u32[]{:S(2)}, u32[]{:S(2)}) collective-permute-start(bf16[16,16,128]{2,1,0:T(8,128)(2,1)S(1)} %get-tuple-element.34), channel_id=1, source_target_pairs={{480,2},{224,3},{320,6},{64,7},{256,10},{0,11},{192,12},{448,13},{... | collective-permute-start | bytes 196616 | tf_op jit(solution)/shard_map/ppermute | solution.py:323
  54.3 0.0 collective-permute-done.2.start_two
  54.3 11.0 %collective-permute-done.1.start = bf16[16,16,128]{2,1,0:T(8,128)(2,1)S(1)} collective-permute-done((bf16[16,16,128]{2,1,0:T(8,128)(2,1)S(1)}, bf16[16,16,128]{2,1,0:T(8,128)(2,1)S(1)}, u32[]{:S(2)}, u32[]{:S(2)}) %collective-permute-start.1) | collective-permute-done | bytes 65568 | tf_op jit(solution)/shard_map/ppermute | solution.py:323
  65.3 1.1 %final_kernel.1 = (bf16[128,512]{1,0:T(8,128)(2,1)}, bf16[128,512]{1,0:T(8,128)(2,1)}, bf16[128,512]{1,0:T(8,128)(2,1)}, bf16[1,256,256]{2,1,0:T(8,128)(2,1)}) custom-call(f32[56,128]{1,0:T(8,128)S(1)} %copy-done.3, bf16[128,512]{1,0:T(8,128)(2,1)S(1)} %copy-done, bf16[128,512]{1,0:T(8,128)(2,1)S(1)} %copy-done.1, bf16[128,512]{1,0:T(8,128)(2,1)S(1)} %copy-done.2, ...), custom_call_target="tpu_custom_call" | custom-call | flops 67108864 | bytes 2519040 | tf_op jit(solution)/shard_map/final_kernel/pallas_call | solution.py:257
  (12 shorter events, 0.0 us)
Async XLA Ops:
  0.6 14.9 %copy-start.8 = (bf16[1,256,256]{2,1,0:T(8,128)(2,1)S(1)}, bf16[1,256,256]{2,1,0:T(8,128)(2,1)}, u32[]{:S(2)}) copy-start(bf16[1,256,256]{2,1,0:T(8,128)(2,1)} %rg.1) | copy-start | bytes 393220
  2.8 12.8 %copy-start.3 = (f32[56,128]{1,0:T(8,128)S(1)}, f32[56,128]{1,0:T(8,128)}, u32[]{:S(2)}) copy-start(f32[56,128]{1,0:T(8,128)} %get-tuple-element.24.rates) | copy-start | bytes 86020
  2.8 12.8 %copy-start.4 = (bf16[1,256,256]{2,1,0:T(8,128)(2,1)S(1)}, bf16[1,256,256]{2,1,0:T(8,128)(2,1)}, u32[]{:S(2)}) copy-start(bf16[1,256,256]{2,1,0:T(8,128)(2,1)} %rq.3) | copy-start | bytes 393220
  2.8 18.6 %copy-start.2 = (bf16[128,512]{1,0:T(8,128)(2,1)S(1)}, bf16[128,512]{1,0:T(8,128)(2,1)}, u32[]{:S(2)}) copy-start(bf16[128,512]{1,0:T(8,128)(2,1)} %pg.3) | copy-start | bytes 393220
  2.8 18.6 %copy-start.5 = (bf16[128,512]{1,0:T(8,128)(2,1)S(1)}, bf16[128,512]{1,0:T(8,128)(2,1)}, u32[]{:S(2)}) copy-start(bf16[128,512]{1,0:T(8,128)(2,1)} %pq.1) | copy-start | bytes 393220
  2.8 24.2 %all-to-all-start = ((bf16[32,32,128]{2,1,0:T(8,128)(2,1)}), bf16[32,32,128]{2,1,0:T(8,128)(2,1)S(1)}, u32[]{:S(2)}, u32[]{:S(2)}) async-start(bf16[32,32,128]{2,1,0:T(8,128)(2,1)} %bitcast.1), calls=%async_computation | async-start | bytes 524288 | tf_op jit(solution)/shard_map/all_to_all | solution.py:306
  15.6 5.8 %copy-start = (bf16[128,512]{1,0:T(8,128)(2,1)S(1)}, bf16[128,512]{1,0:T(8,128)(2,1)}, u32[]{:S(2)}) copy-start(bf16[128,512]{1,0:T(8,128)(2,1)} %pk.3) | copy-start | bytes 393220
  15.6 5.8 %copy-start.1 = (bf16[128,512]{1,0:T(8,128)(2,1)S(1)}, bf16[128,512]{1,0:T(8,128)(2,1)}, u32[]{:S(2)}) copy-start(bf16[128,512]{1,0:T(8,128)(2,1)} %pv.3) | copy-start | bytes 393220
  15.9 6.6 %copy-start.6 = (bf16[1,256,256]{2,1,0:T(8,128)(2,1)S(1)}, bf16[1,256,256]{2,1,0:T(8,128)(2,1)}, u32[]{:S(2)}) copy-start(bf16[1,256,256]{2,1,0:T(8,128)(2,1)} %rk.1) | copy-start | bytes 393220
  15.9 6.6 %copy-start.7 = (bf16[1,256,256]{2,1,0:T(8,128)(2,1)S(1)}, bf16[1,256,256]{2,1,0:T(8,128)(2,1)}, u32[]{:S(2)}) copy-start(bf16[1,256,256]{2,1,0:T(8,128)(2,1)} %rv.1) | copy-start | bytes 393220
  15.9 11.1 %collective-permute-start = (bf16[16,16,128]{2,1,0:T(8,128)(2,1)S(1)}, bf16[16,16,128]{2,1,0:T(8,128)(2,1)S(1)}, u32[]{:S(2)}, u32[]{:S(2)}) collective-permute-start(bf16[16,16,128]{2,1,0:T(8,128)(2,1)S(1)} %get-tuple-element.26), channel_id=1, source_target_pairs={{0,160},{1,384},{2,320},{3,224},{4,128},{5,416},{6,288},{7,192},{8... | collective-permute-start | bytes 196616 | tf_op jit(solution)/shard_map/ppermute | solution.py:307
  47.1 18.2 %all-to-all-start.2 = ((bf16[32,32,128]{2,1,0:T(8,128)(2,1)}), bf16[32,32,128]{2,1,0:T(8,128)(2,1)S(1)}, u32[]{:S(2)}, u32[]{:S(2)}) async-start(bf16[32,32,128]{2,1,0:T(8,128)(2,1)} %get-tuple-element.30), calls=%async_computation.2 | async-start | bytes 524288 | tf_op jit(solution)/shard_map/all_to_all | solution.py:322
  51.4 3.0 %collective-permute-start.2 = (bf16[16,16,128]{2,1,0:T(8,128)(2,1)S(1)}, bf16[16,16,128]{2,1,0:T(8,128)(2,1)S(1)}, u32[]{:S(2)}, u32[]{:S(2)}) collective-permute-start(bf16[16,16,128]{2,1,0:T(8,128)(2,1)S(1)} %get-tuple-element.34), channel_id=1, source_target_pairs={{224,0},{480,1},{32,4},{288,5},{0,8},{256,9},{240,16},{496,17},{48... | collective-permute-start | bytes 196616 | tf_op jit(solution)/shard_map/ppermute | solution.py:323
  52.1 13.3 %collective-permute-start.1 = (bf16[16,16,128]{2,1,0:T(8,128)(2,1)S(1)}, bf16[16,16,128]{2,1,0:T(8,128)(2,1)S(1)}, u32[]{:S(2)}, u32[]{:S(2)}) collective-permute-start(bf16[16,16,128]{2,1,0:T(8,128)(2,1)S(1)} %get-tuple-element.34), channel_id=1, source_target_pairs={{480,2},{224,3},{320,6},{64,7},{256,10},{0,11},{192,12},{448,13},{... | collective-permute-start | bytes 196616 | tf_op jit(solution)/shard_map/ppermute | solution.py:323
